TPU v7x, 32 devices: a whole 2x2x4 slice. The times are simulated.
32 devices in a mesh: groups: 2 (over y), rows: 4 (over z), cols: 2 (over x), sub: 2 (over core).
Axes of the slice: x: 2, y: 2, z: 4, core: 2. Of those that a mesh axis runs over, the one named last changes fastest.
Arguments:
- activations: float32 [2048, 8192], P(('groups', 'rows', 'sub'), 'cols'), parts along dimension 0, may hold values from -72 to 72
- plan: int32 [2, 32], replicated, may hold values from 0 to 31, as said below
Outputs:
- rotated: float32 [2048, 8192], P(('groups', 'rows', 'sub'), 'cols'), parts along dimension 0
There are 2 independent parts, one for each index of `groups`. A program takes and returns all parts, laid end to end along the dimension named above; an argument that names none is the same for every part. Nothing has to cross between parts.
Inputs may be any that keep to these rules, and one draw needn't show every extreme that they name: `plan`: each row is a permutation of the blocks. In row 0 the slots j*16 to (j+1)*16 - 1 hold exactly the blocks numbered j*16 to (j+1)*16 - 1. Row r+1 follows row r by the round-robin move: new slot 0 takes old slot 0, new slot 2 takes old slot 1, new slot 2k (k >= 2) takes old slot 2k-2, new slot 2k+1 takes old slot 2k+3 for k < 15, and new slot 31 takes old slot 30.
All inputs are finite; a program needn't handle non-finite values.
Results may differ from a plain program's by a relative error of at most 0.0014.
Values sent between devices are 32-bit elements; how exact they have to be, the bound alone decides.
No kernel may reach another device: no remote copies, remote signals or barrier semaphores. Data moves between devices by JAX's collectives and lax.ppermute only.
A program may use at most 64 MiB of HBM per device.

v0:
```python
import jax
import jax.numpy as jnp
from jax import lax
from jax.sharding import PartitionSpec as P

BLK = 256
ROUNDS = 2


epsilon = 1e-06


def passed_along(block, axis, distance):
    devices = range(lax.axis_size(axis))
    route = [(i - distance, i) for i in devices if i - distance in devices]
    return lax.ppermute(block, axis, route)


def correlate(cross, upper_sq, lower_sq):
    return (
        cross
        * lax.rsqrt(upper_sq + epsilon)[:, :, None]
        * lax.rsqrt(lower_sq + epsilon)[:, None, :]
    )


def own_factors(corr, group_count, group_index):
    high = lax.Precision.HIGHEST
    ident = jnp.eye(corr.shape[1], dtype=jnp.float32)
    left_mats = ident + jnp.einsum("pik,pjk->pij", corr, corr, precision=high)
    right_mats = ident + jnp.einsum("pki,pkj->pij", corr, corr, precision=high)
    matrices = jnp.concatenate([left_mats, right_mats], axis=0)
    total = matrices.shape[0]
    per_device = max(1, -(-total // group_count))
    picks = (group_index * per_device + jnp.arange(per_device, dtype=jnp.int32)) % total
    chosen = jnp.take(matrices, picks, axis=0)
    factors = jnp.linalg.cholesky(chosen)
    invert = jax.vmap(lambda factor: jax.scipy.linalg.solve_triangular(factor, ident, lower=True))
    return invert(factors)


def apply_rotation(corr, inverses, upper, lower):
    high = lax.Precision.HIGHEST
    pair_total = corr.shape[0]
    left_inv = inverses[:pair_total]
    right_inv = inverses[pair_total : 2 * pair_total]
    mixed_upper = upper + jnp.einsum("tpk,pik->tpi", lower, corr, precision=high)
    mixed_lower = lower - jnp.einsum("tpk,pkj->tpj", upper, corr, precision=high)
    new_upper = jnp.einsum("tpk,pjk->tpj", mixed_upper, left_inv, precision=high)
    new_lower = jnp.einsum("tpk,pjk->tpj", mixed_lower, right_inv, precision=high)
    return (new_upper, new_lower)


def local_terms(upper, lower):
    cross = jnp.einsum("tpi,tpj->pij", upper, lower, precision=lax.Precision.HIGHEST)
    return (cross, jnp.sum(upper * upper, axis=0), jnp.sum(lower * lower, axis=0))


def on_device(activations, plan):
    row_count = activations.shape[0]
    block_count = activations.shape[1] // BLK
    column = lax.axis_index("cols")
    final_column = lax.axis_size("cols") - 1
    local_order = (
        lax.dynamic_slice_in_dim(plan[0], column * block_count, block_count) - column * block_count
    )
    slotted = jnp.take(activations.reshape(row_count, block_count, BLK), local_order, axis=1)
    upper = slotted[:, 0::2]
    lower = slotted[:, 1::2]
    first = column == 0
    final = column == final_column
    token_group = lax.axis_size(("rows", "sub"))
    token_index = lax.axis_index(("rows", "sub"))
    for round_index in range(ROUNDS):
        cross, upper_sq, lower_sq = lax.psum(local_terms(upper, lower), ("rows", "sub"))
        corr = correlate(cross, upper_sq, lower_sq)
        mine = own_factors(corr, token_group, token_index)
        inverses = lax.all_gather(mine, ("rows", "sub"), axis=0, tiled=True)
        upper, lower = apply_rotation(corr, inverses, upper, lower)
        if round_index + 1 < ROUNDS:
            carried = jnp.where(first, upper.at[:, 0].set(lower[:, 0]), upper)
            arriving = passed_along(carried[:, -1], "cols", 1)
            arriving = jnp.where(first, upper[:, 0], arriving)
            upper_next = jnp.concatenate([arriving[:, None], carried[:, :-1]], axis=1)
            leaving = passed_along(lower[:, 0], "cols", -1)
            leaving = jnp.where(final, upper[:, -1], leaving)
            lower_next = jnp.concatenate([lower[:, 1:], leaving[:, None]], axis=1)
            upper = upper_next
            lower = lower_next
    return jnp.stack([upper, lower], axis=2).reshape(row_count, block_count * BLK)


def solution(mesh):
    in_specs = (P(("groups", "rows", "sub"), "cols"), P())
    out_specs = P(("groups", "rows", "sub"), "cols")
    return jax.shard_map(
        on_device, mesh=mesh, in_specs=in_specs, out_specs=out_specs, check_vma=False
    )
```

profile of v0, /device:TPU:0, one launch (start us, length us, event | category | flops | bytes accessed | tf_op | source)
XLA Modules:
  0.0 578.2 jit_solution(13132511642743006040)
XLA Ops:
  19.6 31.3 %all-reduce.2 = (f32[8,256]{1,0:T(8,128)S(1)}, f32[8,256]{1,0:T(8,128)S(1)}) all-reduce(f32[8,256]{1,0:T(8,128)S(1)} %get-tuple-element.37, f32[8,256]{1,0:T(8,128)S(1)} %get-tuple-element.36), channel_id=1, replica_groups=mesh['groups'=2,'rows'=4,'cols'=2,'sub'=2] {'rows','sub'}, use_global_device_ids=true, to_apply=%region_4.5 | all-reduce | flops 4096 | bytes 32768 | tf_op jit(solution)/shard_map/psum | solution.py:75
  51.1 36.4 %all-reduce.6.cloned.1.call-done = f32[8,256,256]{2,1,0:T(8,128)} async-done(((f32[8,256,256]{2,1,0:T(8,128)}), f32[8,256,256]{2,1,0:T(8,128)}) %all-reduce.6.cloned.1.call-update) | async-done | bytes 2097168 | tf_op jit(solution)/shard_map/psum | solution.py:75
  87.4 6.5 %convolution_add_fusion.2 = f32[8,256,256]{2,1,0:T(8,128)S(1)} fusion(f32[8,256,256]{2,1,0:T(8,128)} %all-reduce.6.cloned.1.call-done, f32[8,256]{1,0:T(8,128)S(1)} %get-tuple-element.78, f32[8,256]{1,0:T(8,128)S(1)} %get-tuple-element.79, f32[256,256]{1,0:T(8,128)S(1)} %fusion.28), kind=kOutput, calls=%fused_computation.15 | convolution fusion | flops 1612185600 | bytes 4472832 | tf_op jit(solution)/shard_map/pki,pkj->pij/dot_general | solution.py:31
  108.4 23.5 %custom-call.17 = f32[2,128,128]{2,1,0:T(8,128)S(1)} custom-call(f32[2,128,128]{2,1,0:T(8,128)S(1)} %cholesky.198), custom_call_target="Cholesky" | custom-call | tf_op jit(solution)/shard_map/jit(cholesky)/cholesky | solution.py:37
  131.9 20.5 %custom-call.18 = f32[2,1,128,128]{2,3,1,0:T(8,128)} custom-call(f32[2,1,128,128]{3,2,1,0:T(8,128)S(1)} %select_bitcast_fusion.2), custom_call_target="InvertDiagBlocksLowerTriangular" | custom-call | tf_op jit(solution)/shard_map/jit(cholesky)/cholesky | solution.py:37
  155.7 24.3 %custom-call.19 = f32[2,128,128]{2,1,0:T(8,128)S(1)} custom-call(f32[2,128,128]{2,1,0:T(8,128)} %convolution_subtract_fusion.3), custom_call_target="Cholesky" | custom-call | tf_op jit(solution)/shard_map/jit(cholesky)/cholesky | solution.py:37
  182.1 4.0 while.5
  186.1 40.0 %custom-call.20 = f32[2,2,128,128]{2,3,1,0:T(8,128)} custom-call(f32[2,2,128,128]{3,2,1,0:T(8,128)S(1)} %bitcast.148), custom_call_target="InvertDiagBlocksLowerTriangular" | custom-call | tf_op jit(solution)/shard_map/vmap(jit(_solve_triangular))/triangular_solve | solution.py:38
  230.4 5.2 fusion.3
  238.2 38.7 %all-gather.3.cloned.1.call-done = f32[16,256,256]{2,1,0:T(8,128)} async-done(((f32[2,256,256]{2,1,0:T(8,128)}), f32[16,256,256]{2,1,0:T(8,128)}) %all-gather.3.cloned.1.call-update) | async-done | bytes 4194320 | tf_op jit(solution)/shard_map/all_gather | solution.py:78
  276.9 4.3 fusion.58
  285.9 4.0 collective-permute-start
  292.9 4.5 collective-permute-done.1
  301.7 27.0 %all-reduce.1 = (f32[8,256]{1,0:T(8,128)S(1)}, f32[8,256]{1,0:T(8,128)S(1)}) all-reduce(f32[8,256]{1,0:T(8,128)S(1)} %multiply_reduce_fusion, f32[8,256]{1,0:T(8,128)S(1)} %multiply_reduce_fusion.1), channel_id=1, replica_groups=mesh['groups'=2,'rows'=4,'cols'=2,'sub'=2] {'rows','sub'}, use_global_device_ids=true, to_apply=%region_13.17 | all-reduce | flops 4096 | bytes 32768 | tf_op jit(solution)/shard_map/psum | solution.py:75
  328.7 35.9 %all-reduce.8.cloned.1.call-done = f32[8,256,256]{2,1,0:T(8,128)} async-done(((f32[8,256,256]{2,1,0:T(8,128)}), f32[8,256,256]{2,1,0:T(8,128)}) %all-reduce.8.cloned.1.call-update) | async-done | bytes 2097168 | tf_op jit(solution)/shard_map/psum | solution.py:75
  364.6 6.5 %convolution_add_fusion = f32[8,256,256]{2,1,0:T(8,128)S(1)} fusion(f32[8,256,256]{2,1,0:T(8,128)} %all-reduce.8.cloned.1.call-done, f32[8,256]{1,0:T(8,128)S(1)} %add_rsqrt_fusion, f32[8,256]{1,0:T(8,128)S(1)} %add_rsqrt_fusion.1, f32[256,256]{1,0:T(8,128)S(1)} %fusion.28), kind=kOutput, calls=%fused_computation.13 | convolution fusion | flops 1612185600 | bytes 4472832 | tf_op jit(solution)/shard_map/pki,pkj->pij/dot_general | solution.py:31
  386.4 23.5 %custom-call.21 = f32[2,128,128]{2,1,0:T(8,128)S(1)} custom-call(f32[2,128,128]{2,1,0:T(8,128)S(1)} %cholesky.201), custom_call_target="Cholesky" | custom-call | tf_op jit(solution)/shard_map/jit(cholesky)/cholesky | solution.py:37
  410.6 20.5 %custom-call.22 = f32[2,1,128,128]{2,3,1,0:T(8,128)} custom-call(f32[2,1,128,128]{3,2,1,0:T(8,128)S(1)} %select_bitcast_fusion.1), custom_call_target="InvertDiagBlocksLowerTriangular" | custom-call | tf_op jit(solution)/shard_map/jit(cholesky)/cholesky | solution.py:37
  435.3 24.9 %custom-call.23 = f32[2,128,128]{2,1,0:T(8,128)} custom-call(f32[2,128,128]{2,1,0:T(8,128)} %convolution_subtract_fusion.2), custom_call_target="Cholesky" | custom-call | tf_op jit(solution)/shard_map/jit(cholesky)/cholesky | solution.py:37
  463.9 6.6 %while.6 = (s32[]{:T(128)}, f32[2,256,256]{2,1,0:T(8,128)S(1)}, s32[2,2]{1,0:T(2,128)}, f32[2,2,128,128]{3,2,0,1:T(8,128)}, s32[]{:T(128)}) while((s32[]{:T(128)}, f32[2,256,256]{2,1,0:T(8,128)S(1)}, s32[2,2]{1,0:T(2,128)}, f32[2,2,128,128]{3,2,0,1:T(8,128)}, s32[]{:T(128)}) %tuple.66), condition=%wide.while_cond.1.clone, body=%wide.while_body.1.clone.sunk | while | flops 2 | bytes 263277 | solution.py:38
  470.4 41.0 %custom-call.24 = f32[2,2,128,128]{2,3,1,0:T(8,128)} custom-call(f32[2,2,128,128]{3,2,1,0:T(8,128)} %bitcast.147), custom_call_target="InvertDiagBlocksLowerTriangular" | custom-call | tf_op jit(solution)/shard_map/vmap(jit(_solve_triangular))/triangular_solve | solution.py:38
  516.4 4.7 fusion.1
  523.8 39.5 %all-gather.5.cloned.1.call-done = f32[16,256,256]{2,1,0:T(8,128)} async-done(((f32[2,256,256]{2,1,0:T(8,128)}), f32[16,256,256]{2,1,0:T(8,128)}) %all-gather.5.cloned.1.call-update) | async-done | bytes 4194320 | tf_op jit(solution)/shard_map/all_gather | solution.py:78
  563.3 3.9 convolution_bitcast_fusion
  (163 shorter events, 97.7 us)
Async XLA Ops:
  6.5 80.9 %all-reduce.6.cloned.1.call-start = ((), (), s32[]{:S(2)}) async-start(), calls=%async_computation | async-start | bytes 4194304 | tf_op jit(solution)/shard_map/psum | solution.py:75
  19.3 257.6 %all-gather.3.cloned.1.call-start = ((), (), s32[]{:S(2)}) async-start(), calls=%async_computation.1 | async-start | bytes 4718592 | tf_op jit(solution)/shard_map/all_gather | solution.py:78
  19.4 87.1 %copy-start.26 = (pred[2]{0:T(512)(128)(4,1)}, pred[2]{0:T(512)(128)(4,1)S(1)}, u32[]{:S(2)}) copy-start(pred[2]{0:T(512)(128)(4,1)S(1)} %compare_and_fusion) | copy-start | bytes 10
  50.9 47.9 %copy-start.27 = (s32[1024]{0:T(1024)}, s32[1024]{0:T(1024)S(1)}, u32[]{:S(2)}) copy-start(s32[1024]{0:T(1024)S(1)} %pad_clamp_fusion) | copy-start | bytes 12292
  50.9 81.0 %copy-start.25 = (pred[128,128]{1,0:T(8,128)(4,1)}, pred[128,128]{1,0:T(8,128)(4,1)S(1)}, u32[]{:S(2)}) copy-start(pred[128,128]{1,0:T(8,128)(4,1)S(1)} %iota_compare_fusion.3) | copy-start | bytes 49156
  50.9 129.0 %copy-start.24 = (pred[128,128]{1,0:T(8,128)(4,1)}, pred[128,128]{1,0:T(8,128)(4,1)S(1)}, u32[]{:S(2)}) copy-start(pred[128,128]{1,0:T(8,128)(4,1)S(1)} %iota_compare_fusion.2) | copy-start | bytes 49156
  51.0 129.8 %copy-start.23 = (pred[256,256]{1,0:T(8,128)(4,1)}, pred[256,256]{1,0:T(8,128)(4,1)S(1)}, u32[]{:S(2)}) copy-start(pred[256,256]{1,0:T(8,128)(4,1)S(1)} %iota_compare_fusion) | copy-start | bytes 196612
  51.0 175.0 %copy-start.22 = (f32[128,256]{1,0:T(8,128)}, f32[128,256]{1,0:T(8,128)S(1)}, u32[]{:S(2)}) copy-start(f32[128,256]{1,0:T(8,128)S(1)} %get-tuple-element.71) | copy-start | bytes 393220
  51.1 176.3 %copy-start.21 = (f32[128,256]{1,0:T(8,128)}, f32[128,256]{1,0:T(8,128)S(1)}, u32[]{:S(2)}) copy-start(f32[128,256]{1,0:T(8,128)S(1)} %get-tuple-element.70) | copy-start | bytes 393220
  87.4 6.5 %copy-start.2 = (f32[8,256,256]{2,1,0:T(8,128)S(1)}, f32[8,256,256]{2,1,0:T(8,128)}, u32[]{:S(2)}) copy-start(f32[8,256,256]{2,1,0:T(8,128)} %all-reduce.6.cloned.1.call-done) | copy-start | bytes 6291460
  186.1 49.6 %copy-start.28 = (s32[2,2]{1,0:T(2,128)}, s32[2,2]{1,0:T(2,128)S(1)}, u32[]{:S(2)}) copy-start(s32[2,2]{1,0:T(2,128)S(1)} %get-tuple-element.188) | copy-start | bytes 52
  230.0 134.6 %all-reduce.8.cloned.1.call-start = ((), (), s32[]{:S(2)}) async-start(), calls=%async_computation.2 | async-start | bytes 4194304 | tf_op jit(solution)/shard_map/psum | solution.py:75
  230.4 5.2 copy-start.3
  276.9 4.4 copy-start
  284.8 6.4 %copy-start.8 = (f32[128,8,256]{2,0,1:T(8,128)}, f32[128,8,256]{2,0,1:T(8,128)S(1)}, u32[]{:S(2)}) copy-start(f32[128,8,256]{2,0,1:T(8,128)S(1)} %convolution_bitcast_fusion.2) | copy-start | bytes 3145732
  285.9 6.9 %collective-permute-start = (f32[128,256]{1,0:T(8,128)S(1)}, f32[128,256]{1,0:T(8,128)}, u32[]{:S(2)}, u32[]{:S(2)}) collective-permute-start(f32[128,256]{1,0:T(8,128)S(1)} %slice_bitcast_fusion.5), channel_id=1, source_target_pairs={{0,2},{1,3},{4,6},{5,7},{8,10},{9,11},{12,14},{13,15},{16,18},{17,... | collective-permute-start | bytes 393224 | tf_op jit(solution)/shard_map/ppermute | solution.py:16
  290.0 7.4 %collective-permute-start.1 = (f32[128,256]{1,0:T(8,128)S(1)}, f32[128,256]{1,0:T(8,128)}, u32[]{:S(2)}, u32[]{:S(2)}) collective-permute-start(f32[128,256]{1,0:T(8,128)S(1)} %get-tuple-element.69), channel_id=1, source_target_pairs={{2,0},{3,1},{6,4},{7,5},{10,8},{11,9},{14,12},{15,13},{18,16},{19,... | collective-permute-start | bytes 393224 | tf_op jit(solution)/shard_map/ppermute | solution.py:16
  292.8 8.7 %copy-start.5 = (f32[128,7,256]{2,0,1:T(8,128)}, f32[128,7,256]{2,0,1:T(8,128)S(1)}, u32[]{:S(2)}) copy-start(f32[128,7,256]{2,0,1:T(8,128)S(1)} %slice.136) | copy-start | bytes 2752516
  298.3 3.4 copy-start.14
  301.5 261.8 %all-gather.5.cloned.1.call-start = ((), (), s32[]{:S(2)}) async-start(), calls=%async_computation.3 | async-start | bytes 4718592 | tf_op jit(solution)/shard_map/all_gather | solution.py:78
  364.6 6.5 %copy-start.4 = (f32[8,256,256]{2,1,0:T(8,128)S(1)}, f32[8,256,256]{2,1,0:T(8,128)}, u32[]{:S(2)}) copy-start(f32[8,256,256]{2,1,0:T(8,128)} %all-reduce.8.cloned.1.call-done) | copy-start | bytes 6291460
  516.4 4.7 copy-start.6
  523.8 43.5 %copy-start.7 = (f32[128,8,256]{2,0,1:T(8,128)S(1)}, f32[128,8,256]{2,0,1:T(8,128)}, u32[]{:S(2)}) copy-start(f32[128,8,256]{2,0,1:T(8,128)} %fusion.1) | copy-start | bytes 3145732
  563.3 4.0 copy-start.1
  (11 other events, 15.5 us)
Sparse Core Ops, SparseCore 0:
  19.4 67.9 all-reduce.5
  230.1 46.7 all-gather.2
  301.6 62.9 all-reduce.7
  516.5 46.7 all-gather.4
where the time goes:
time: 582 us; the launch traced here: 578 us
  other arithmetic  237 us (41%)
  waiting for transfers between devices  155 us (27%)
  matrix products  65.6 us (11%)
  blocking collectives  58.2 us (10%)
  local copies, waits for them, and re-layouts  42.1 us (7%)
  between operations  14.1 us (2%)
  starting transfers between devices  5.84 us (1%)
    another operation x18, other arithmetic, own_factors(): factors = jnp.linalg.cholesky(chosen)  139 us
    another operation x8, other arithmetic, own_factors(): jax.scipy.linalg.solve_triangular(factor, ident, lower=True)  85 us
    all_gather x2, waiting for transfers between devices, on_device(): inverses = lax.all_gather(mine, ('rows', 'sub'), axis=0, tiled=True)  78.2 us
    psum x2, waiting for transfers between devices, on_device(): lax.psum(local_terms(upper, lower), ('rows', 'sub'))  72.2 us
    psum x2, blocking collectives, on_device(): lax.psum(local_terms(upper, lower), ('rows', 'sub'))  58.2 us
    dot_general x2, matrix products, own_factors(): right_mats = ident + jnp.einsum('pki,pkj->pij', corr, corr, precision=high)  13 us
  transfers between devices with their start and end apart: 6, of which 5 were waited for; matrix products, arithmetic and copies ran while one was open for 3% of the time, Pallas kernels for 0%

commit v1 on v0

v1 whole, which is shorter than its diff:
```python
import functools

import jax
import jax.numpy as jnp
from jax import lax
from jax.experimental import pallas as pl
from jax.experimental.pallas import tpu as pltpu
from jax.sharding import PartitionSpec as P

BLK = 256
ROUNDS = 2
PANEL = 64
SUBLANES = 8

epsilon = 1e-06
HIGH = lax.Precision.HIGHEST
VMEM_LIMIT = 40 * 1024 * 1024


def contract(a, b, a_dim, b_dim):
    return lax.dot_general(
        a, b, (((a_dim,), (b_dim,)), ((), ())), precision=HIGH, preferred_element_type=jnp.float32
    )


def iota2(shape, dim):
    return lax.broadcasted_iota(jnp.int32, shape, dim)


def eliminate(blocks):
    width = 2 * PANEL
    tiles = PANEL // SUBLANES
    ident = jnp.where(iota2((PANEL, PANEL), 0) == iota2((PANEL, PANEL), 1), 1.0, 0.0).astype(jnp.float32)
    parts = []
    for block in blocks:
        whole = jnp.concatenate([block, ident], axis=1)
        parts.append([whole[SUBLANES * v : SUBLANES * (v + 1)] for v in range(tiles)])
    sub = iota2((SUBLANES, width), 0)
    for j in range(PANEL):
        home, line = divmod(j, SUBLANES)
        for part in parts:
            row = part[home][line : line + 1, :]
            scaled = row / row[:, j : j + 1]
            for v in range(home, tiles):
                column = part[v][:, j : j + 1]
                step = column * scaled
                if v == home:
                    step = jnp.where(sub > line, step, 0.0)
                part[v] = part[v] - step
    outs = []
    on_diagonal = iota2((PANEL, width), 0) == iota2((PANEL, width), 1)
    for part in parts:
        whole = jnp.concatenate(part, axis=0)
        pivots = jnp.sum(jnp.where(on_diagonal, whole, 0.0), axis=1, keepdims=True)
        outs.append(whole[:, PANEL:] * lax.rsqrt(pivots))
    return outs


def inverse_factors(aug_ref):
    for p in range(BLK // PANEL):
        top = p * PANEL
        end = top + PANEL
        blocks = [aug_ref[m, top:end, top:end] for m in range(2)]
        invs = eliminate(blocks)
        for m in range(2):
            rows = contract(invs[m], aug_ref[m, top:end, :], 1, 0)
            aug_ref[m, top:end, BLK:] = rows[:, BLK:]
            if end < BLK:
                aug_ref[m, end:, :] = aug_ref[m, end:, :] - contract(rows[:, end:BLK], rows, 0, 0)


def rotate_pair(upper_ref, lower_ref, cross, upper_sq, lower_sq, aug_ref):
    square = (BLK, BLK)
    diagonal = iota2(square, 0) == iota2(square, 1)
    ident = jnp.where(diagonal, 1.0, 0.0).astype(jnp.float32)
    upper_sq = jnp.sum(
        jnp.where(diagonal, jnp.broadcast_to(upper_sq, square), 0.0), axis=1, keepdims=True
    )
    corr = cross * lax.rsqrt(upper_sq + epsilon) * lax.rsqrt(lower_sq + epsilon)
    aug_ref[0, :, :BLK] = ident + contract(corr, corr, 1, 1)
    aug_ref[1, :, :BLK] = ident + contract(corr, corr, 0, 0)
    aug_ref[0, :, BLK:] = ident
    aug_ref[1, :, BLK:] = ident
    inverse_factors(aug_ref)
    upper = upper_ref[...]
    lower = lower_ref[...]
    mixed_upper = upper + contract(lower, corr, 1, 1)
    mixed_lower = lower - contract(upper, corr, 1, 0)
    new_upper = contract(mixed_upper, aug_ref[0, :, BLK:], 1, 1)
    new_lower = contract(mixed_lower, aug_ref[1, :, BLK:], 1, 1)
    return new_upper, new_lower


def terms_of(upper, lower):
    return (
        contract(upper, lower, 0, 0),
        jnp.sum(upper * upper, axis=0, keepdims=True),
        jnp.sum(lower * lower, axis=0, keepdims=True),
    )


def pack_kernel(order_ref, x_ref, *refs):
    outs, sem = refs[:-1], refs[-1]
    copies = []
    for i, out in enumerate(outs):
        for half in range(2):
            start = pl.multiple_of(order_ref[2 * i + half] * BLK, BLK)
            copies.append(
                pltpu.make_async_copy(
                    x_ref.at[:, pl.ds(start, BLK)],
                    out.at[:, half * BLK : (half + 1) * BLK],
                    sem.at[2 * i + half],
                )
            )
    for copy in copies:
        copy.start()
    for copy in copies:
        copy.wait()


def pack(order, x, count):
    rows = x.shape[0]
    piece = jax.ShapeDtypeStruct((rows, 2 * BLK), jnp.float32)
    return pl.pallas_call(
        pack_kernel,
        out_shape=[piece] * count,
        in_specs=[pl.BlockSpec(memory_space=pltpu.SMEM), pl.BlockSpec(memory_space=pl.ANY)],
        out_specs=[pl.BlockSpec(memory_space=pl.ANY)] * count,
        scratch_shapes=[pltpu.SemaphoreType.DMA((2 * count,))],
        name="pack",
    )(order, x)


def unpack_kernel(place_ref, *refs):
    pieces, out_ref, sem = refs[:-2], refs[-2], refs[-1]
    width = 2 * BLK
    copies = []
    for i, piece in enumerate(pieces):
        start = pl.multiple_of(place_ref[i] * width, width)
        copies.append(pltpu.make_async_copy(piece, out_ref.at[:, pl.ds(start, width)], sem.at[i]))
    for copy in copies:
        copy.start()
    for copy in copies:
        copy.wait()


def unpack(place, pieces):
    rows, width = pieces[0].shape
    count = len(pieces)
    return pl.pallas_call(
        unpack_kernel,
        out_shape=jax.ShapeDtypeStruct((rows, count * width), jnp.float32),
        in_specs=[pl.BlockSpec(memory_space=pltpu.SMEM)]
        + [pl.BlockSpec(memory_space=pl.ANY)] * count,
        out_specs=pl.BlockSpec(memory_space=pl.ANY),
        scratch_shapes=[pltpu.SemaphoreType.DMA((count,))],
        name="unpack",
    )(place, *pieces)


def first_kernel(count, given, source_ref, *refs):
    pieces = refs[:count]
    refs = refs[count:]
    terms, refs = refs[: 3 * given], refs[3 * given :]
    new_upper_ref, new_lower_ref, upper_ref, lower_ref, aug_ref, sem = refs
    rows = pieces[0].shape[0]
    copies = []
    for i, piece in enumerate(pieces):
        start = pl.multiple_of(source_ref[i] * rows, rows)
        for half, target in enumerate((upper_ref, lower_ref)):
            copies.append(
                pltpu.make_async_copy(
                    piece.at[:, half * BLK : (half + 1) * BLK],
                    target.at[pl.ds(start, rows), :],
                    sem.at[2 * i + half],
                )
            )
    for copy in copies:
        copy.start()
    for copy in copies:
        copy.wait()
    if given:
        cross, upper_sq, lower_sq = (term[...] for term in terms)
    else:
        cross, upper_sq, lower_sq = terms_of(upper_ref[...], lower_ref[...])
    new_upper, new_lower = rotate_pair(upper_ref, lower_ref, cross, upper_sq, lower_sq, aug_ref)
    new_upper_ref[...] = new_upper
    new_lower_ref[...] = new_lower


def first_round(source, pieces, terms):
    rows = pieces[0].shape[0]
    count = len(pieces)
    tokens = rows * count
    block = jax.ShapeDtypeStruct((tokens, BLK), jnp.float32)
    vmem = pl.BlockSpec(memory_space=pltpu.VMEM)
    return pl.pallas_call(
        functools.partial(first_kernel, count, int(bool(terms))),
        out_shape=[block, block],
        in_specs=[pl.BlockSpec(memory_space=pltpu.SMEM)]
        + [pl.BlockSpec(memory_space=pl.ANY)] * count
        + [vmem] * len(terms),
        out_specs=[vmem, vmem],
        scratch_shapes=[
            pltpu.VMEM((tokens, BLK), jnp.float32),
            pltpu.VMEM((tokens, BLK), jnp.float32),
            pltpu.VMEM((2, BLK, 2 * BLK), jnp.float32),
            pltpu.SemaphoreType.DMA((2 * count,)),
        ],
        compiler_params=pltpu.CompilerParams(vmem_limit_bytes=VMEM_LIMIT),
        name="first_round",
    )(source, *pieces, *terms)


def last_kernel(count, given, source_ref, upper_ref, lower_ref, *refs):
    terms, refs = refs[: 3 * given], refs[3 * given :]
    outs = refs[:count]
    result_ref, aug_ref, sem = refs[count:]
    rows = outs[0].shape[0]
    if given:
        cross, upper_sq, lower_sq = (term[...] for term in terms)
    else:
        cross, upper_sq, lower_sq = terms_of(upper_ref[...], lower_ref[...])
    new_upper, new_lower = rotate_pair(upper_ref, lower_ref, cross, upper_sq, lower_sq, aug_ref)
    result_ref[:, :BLK] = new_upper
    result_ref[:, BLK:] = new_lower
    copies = []
    for i, out in enumerate(outs):
        start = pl.multiple_of(source_ref[i] * rows, rows)
        copies.append(pltpu.make_async_copy(result_ref.at[pl.ds(start, rows), :], out, sem.at[i]))
    for copy in copies:
        copy.start()
    for copy in copies:
        copy.wait()


def last_round(source, upper, lower, terms):
    tokens = upper.shape[0]
    count = source.shape[0]
    piece = jax.ShapeDtypeStruct((tokens // count, 2 * BLK), jnp.float32)
    vmem = pl.BlockSpec(memory_space=pltpu.VMEM)
    return pl.pallas_call(
        functools.partial(last_kernel, count, int(bool(terms))),
        out_shape=[piece] * count,
        in_specs=[pl.BlockSpec(memory_space=pltpu.SMEM), vmem, vmem] + [vmem] * len(terms),
        out_specs=[pl.BlockSpec(memory_space=pl.ANY)] * count,
        scratch_shapes=[
            pltpu.VMEM((tokens, 2 * BLK), jnp.float32),
            pltpu.VMEM((2, BLK, 2 * BLK), jnp.float32),
            pltpu.SemaphoreType.DMA((count,)),
        ],
        compiler_params=pltpu.CompilerParams(vmem_limit_bytes=VMEM_LIMIT),
        name="last_round",
    )(source, upper, lower, *terms)


def on_device(activations, plan):
    token_axes = ("rows", "sub")
    all_axes = ("rows", "cols", "sub")
    subs = lax.axis_size("sub")
    columns = lax.axis_size("cols")
    column = lax.axis_index("cols")
    block_count = activations.shape[1] // BLK
    pairs = block_count // 2
    token_group = lax.axis_size(token_axes)
    token_index = lax.axis_index(token_axes)
    teams = token_group // pairs
    assert teams * pairs == token_group and pairs & (pairs - 1) == 0
    member = token_index % pairs
    shifts = jnp.arange(pairs, dtype=jnp.int32)
    partner = jnp.bitwise_xor(member, shifts)
    backwards = column % 2 == 1

    def pair_of(member):
        return jnp.where(backwards, pairs - 1 - member, member)

    def exchange(pieces):
        arrived = [pieces[0]]
        for shift in range(1, pairs):
            route = [(t, t ^ shift) for t in range(token_group)]
            arrived.append(lax.ppermute(pieces[shift], token_axes, route))
        return arrived

    def added_up(upper, lower):
        groups = [[team * pairs + m for team in range(teams)] for m in range(pairs)]
        total = []
        for term in terms_of(upper, lower):
            full = term
            for step in range(1, teams):
                route = [
                    (group[i], group[(i + step) % teams]) for group in groups for i in range(teams)
                ]
                full = full + lax.ppermute(term, token_axes, route)
            total.append(full)
        return total

    local_order = (
        lax.dynamic_slice_in_dim(plan[0], column * block_count, block_count) - column * block_count
    )
    order = jnp.take(local_order.reshape(pairs, 2), pair_of(partner), axis=0).reshape(-1)
    pieces = exchange(pack(order, activations, pairs))

    terms = []
    if teams > 1:
        canonical = jnp.concatenate(pieces, axis=0)
        terms = added_up(canonical[:, :BLK], canonical[:, BLK:])
    upper, lower = first_round(partner, pieces, terms)

    def device_of(pair):
        home, inner = divmod(pair, pairs)
        return home, pairs - 1 - inner if home % 2 else inner

    total_pairs = columns * pairs
    chain = column * pairs + pair_of(member)
    first = chain == 0
    final = chain == total_pairs - 1

    def along(block, distance):
        route = []
        for pair in range(total_pairs):
            if 0 <= pair + distance < total_pairs:
                for team in range(teams):
                    ends = []
                    for one in (pair, pair + distance):
                        home, inner = device_of(one)
                        row, sub = divmod(team * pairs + inner, subs)
                        ends.append((row * columns + home) * subs + sub)
                    route.append(tuple(ends))
        return lax.ppermute(block, all_axes, route)

    arriving = along(jnp.where(first, lower, upper), 1)
    leaving = along(lower, -1)
    next_upper = jnp.where(first, upper, arriving)
    next_lower = jnp.where(final, upper, leaving)

    terms = added_up(next_upper, next_lower) if teams > 1 else []
    pieces = exchange(last_round(partner, next_upper, next_lower, terms))
    return unpack(pair_of(partner), pieces)


def solution(mesh):
    in_specs = (P(("groups", "rows", "sub"), "cols"), P())
    out_specs = P(("groups", "rows", "sub"), "cols")
    return jax.shard_map(
        on_device, mesh=mesh, in_specs=in_specs, out_specs=out_specs, check_vma=False
    )
```

time: 582 us -> 327 us (0.56)
  the two profiles are of different devices: /device:TPU:0 before, /device:TPU:19 now
where the time goes in v1:
time: 327 us
  Pallas kernels  197 us (60%)
  waiting for transfers between devices  98 us (30%)
  starting transfers between devices  21.1 us (6%)
  local copies, waits for them, and re-layouts  7.54 us (2%)
    ppermute x14, waiting for transfers between devices, exchange(): arrived.append(lax.ppermute(pieces[shift], token_axes, route))  86.3 us
    pallas_call x1, Pallas kernels, pack(): pl.pallas_call(pack_kernel, out_shape=[piece] * count, in_specs=[pl.Block...  65.4 us
    pallas_call x1, Pallas kernels, unpack(): pl.pallas_call(unpack_kernel, out_shape=jax.ShapeDtypeStruct((rows, count...  65.4 us
    pallas_call x1, Pallas kernels, first_round(): pl.pallas_call(functools.partial(first_kernel, count, int(bool(terms))),...  33.3 us
    pallas_call x1, Pallas kernels, last_round(): pl.pallas_call(functools.partial(last_kernel, count, int(bool(terms))), o...  33.2 us
    ppermute x14, starting transfers between devices, exchange(): arrived.append(lax.ppermute(pieces[shift], token_axes, route))  15.5 us
    ppermute x2, waiting for transfers between devices, along(): return lax.ppermute(block, all_axes, route)  11.7 us
  transfers between devices with their start and end apart: 16, of which 12 were waited for; matrix products, arithmetic and copies ran while one was open for 0% of the time, Pallas kernels for 0%

profile of v1, /device:TPU:19, one launch (start us, length us, event | category | flops | bytes accessed | tf_op | source)
XLA Modules:
  0.0 326.8 jit_solution(13041361045281177451)
XLA Ops:
  2.6 65.4 %pack.1 = (f32[128,512]{1,0:T(8,128)}, f32[128,512]{1,0:T(8,128)}, f32[128,512]{1,0:T(8,128)}, f32[128,512]{1,0:T(8,128)}, f32[128,512]{1,0:T(8,128)}, /*index=5...) custom-call(s32[16]{0:T(128)} %select_n.85.order_ref, f32[128,4096]{1,0:T(8,128)} %x_ref.1), custom_call_target="tpu_custom_call" | custom-call | tf_op jit(solution)/shard_map/pack/pallas_call | solution.py:124
  68.8 1.3 collective-permute-start.1
  70.6 2.6 collective-permute-start.4
  73.4 11.2 %collective-permute-done.1.refs_2_ = f32[128,512]{1,0:T(8,128)S(1)} collective-permute-done((f32[128,512]{1,0:T(8,128)}, f32[128,512]{1,0:T(8,128)S(1)}, u32[]{:S(2)}, u32[]{:S(2)}) %collective-permute-start.1) | collective-permute-done | bytes 262176 | tf_op jit(solution)/shard_map/ppermute | solution.py:281
  84.6 2.4 collective-permute-start.6
  87.0 3.2 collective-permute-done.2.refs_3_
  90.2 4.2 %collective-permute-done.4.refs_5_ = f32[128,512]{1,0:T(8,128)S(1)} collective-permute-done((f32[128,512]{1,0:T(8,128)}, f32[128,512]{1,0:T(8,128)S(1)}, u32[]{:S(2)}, u32[]{:S(2)}) %collective-permute-start.4) | collective-permute-done | bytes 262176 | tf_op jit(solution)/shard_map/ppermute | solution.py:281
  94.4 18.9 %collective-permute-done.5.refs_6_ = f32[128,512]{1,0:T(8,128)S(1)} collective-permute-done((f32[128,512]{1,0:T(8,128)}, f32[128,512]{1,0:T(8,128)S(1)}, u32[]{:S(2)}, u32[]{:S(2)}) %collective-permute-start.5) | collective-permute-done | bytes 262176 | tf_op jit(solution)/shard_map/ppermute | solution.py:281
  114.0 5.2 %collective-permute-done.6.refs_7_ = f32[128,512]{1,0:T(8,128)S(1)} collective-permute-done((f32[128,512]{1,0:T(8,128)}, f32[128,512]{1,0:T(8,128)S(1)}, u32[]{:S(2)}, u32[]{:S(2)}) %collective-permute-start.6) | collective-permute-done | bytes 262176 | tf_op jit(solution)/shard_map/ppermute | solution.py:281
  122.7 33.3 %first_round.1 = (f32[1024,256]{1,0:T(8,128)S(1)}, f32[1024,256]{1,0:T(8,128)S(1)}) custom-call(s32[8]{0:T(128)S(1)} %iota_xor_fusion.source_ref, f32[128,512]{1,0:T(8,128)S(1)} %copy-done, f32[128,512]{1,0:T(8,128)S(1)} %collective-permute-done.refs_1_, f32[128,512]{1,0:T(8,128)S(1)} %collective-permute-done.1.refs_2_, ...), custom_call_target="tpu_custom_call" | custom-call | tf_op jit(solution)/shard_map/first_round/pallas_call | solution.py:197
  156.1 2.0 collective-permute-start.7
  158.2 3.5 %collective-permute-start.8 = (f32[1024,256]{1,0:T(8,128)S(1)}, f32[1024,256]{1,0:T(8,128)}, u32[]{:S(2)}, u32[]{:S(2)}) collective-permute-start(f32[1024,256]{1,0:T(8,128)S(1)} %get-tuple-element.32), channel_id=1, source_target_pairs={{1,0},{4,1},{5,4},{8,5},{9,8},{12,9},{13,12},{15,13},{14,15},{11,1... | collective-permute-start | bytes 3145736 | tf_op jit(solution)/shard_map/ppermute | solution.py:329
  161.7 10.9 %collective-permute-done.7 = f32[1024,256]{1,0:T(8,128)} collective-permute-done((f32[1024,256]{1,0:T(8,128)S(1)}, f32[1024,256]{1,0:T(8,128)}, u32[]{:S(2)}, u32[]{:S(2)}) %collective-permute-start.7) | collective-permute-done | bytes 1048608 | tf_op jit(solution)/shard_map/ppermute | solution.py:329
  173.4 1.7 broadcast_select_fusion
  175.2 33.2 %last_round.1 = (f32[128,512]{1,0:T(8,128)S(1)}, f32[128,512]{1,0:T(8,128)S(1)}, f32[128,512]{1,0:T(8,128)S(1)}, f32[128,512]{1,0:T(8,128)S(1)}, f32[128,512]{1,...) custom-call(s32[8]{0:T(128)S(1)} %iota_xor_fusion.source_ref, ...), custom_call_target="tpu_custom_call" | custom-call | tf_op jit(solution)/shard_map/last_round/pallas_call | solution.py:242
  210.1 1.7 collective-permute-start.10
  211.8 3.0 collective-permute-start.13
  214.8 10.6 %collective-permute-done.10.refs_2_ = f32[128,512]{1,0:T(8,128)S(1)} collective-permute-done((f32[128,512]{1,0:T(8,128)S(1)}, f32[128,512]{1,0:T(8,128)S(1)}, u32[]{:S(2)}, u32[]{:S(2)}) %collective-permute-start.10) | collective-permute-done | bytes 262176 | tf_op jit(solution)/shard_map/ppermute | solution.py:281
  225.4 2.0 collective-permute-start.15
  227.4 3.6 %collective-permute-done.11.refs_3_ = f32[128,512]{1,0:T(8,128)S(1)} collective-permute-done((f32[128,512]{1,0:T(8,128)S(1)}, f32[128,512]{1,0:T(8,128)S(1)}, u32[]{:S(2)}, u32[]{:S(2)}) %collective-permute-start.11) | collective-permute-done | bytes 262176 | tf_op jit(solution)/shard_map/ppermute | solution.py:281
  231.0 4.1 %collective-permute-done.13.refs_5_ = f32[128,512]{1,0:T(8,128)S(1)} collective-permute-done((f32[128,512]{1,0:T(8,128)S(1)}, f32[128,512]{1,0:T(8,128)S(1)}, u32[]{:S(2)}, u32[]{:S(2)}) %collective-permute-start.13) | collective-permute-done | bytes 262176 | tf_op jit(solution)/shard_map/ppermute | solution.py:281
  235.1 19.5 %collective-permute-done.14.refs_6_ = f32[128,512]{1,0:T(8,128)S(1)} collective-permute-done((f32[128,512]{1,0:T(8,128)S(1)}, f32[128,512]{1,0:T(8,128)S(1)}, u32[]{:S(2)}, u32[]{:S(2)}) %collective-permute-start.14) | collective-permute-done | bytes 262176 | tf_op jit(solution)/shard_map/ppermute | solution.py:281
  254.6 6.0 %collective-permute-done.15.refs_7_ = f32[128,512]{1,0:T(8,128)S(1)} collective-permute-done((f32[128,512]{1,0:T(8,128)S(1)}, f32[128,512]{1,0:T(8,128)S(1)}, u32[]{:S(2)}, u32[]{:S(2)}) %collective-permute-start.15) | collective-permute-done | bytes 262176 | tf_op jit(solution)/shard_map/ppermute | solution.py:281
  261.3 65.4 %unpack.1 = f32[128,4096]{1,0:T(8,128)} custom-call(s32[8]{0:T(128)} %get-tuple-element.42.place_ref, f32[128,512]{1,0:T(8,128)} %copy-done.1, f32[128,512]{1,0:T(8,128)} %copy-done.6, f32[128,512]{1,0:T(8,128)} %copy-done.7, f32[128,512]{1,0:T(8,128)} %copy-done.8, f32[128,512]{1,0:T(8,128)} %copy-done.9, f32[128,512]{1,0:T(8,128)} %copy-done.10, ...), custom_call_target="tpu_custom_call" | custom-call | tf_op jit(solution)/shard_map/unpack/pallas_call | solution.py:150
  (50 shorter events, 11.5 us)
Async XLA Ops:
  68.1 5.2 %collective-permute-start = (f32[128,512]{1,0:T(8,128)}, f32[128,512]{1,0:T(8,128)S(1)}, u32[]{:S(2)}, u32[]{:S(2)}) collective-permute-start(f32[128,512]{1,0:T(8,128)} %get-tuple-element.24), channel_id=1, source_target_pairs={{0,1},{1,0},{4,5},{5,4},{8,9},{9,8},{12,13},{13,12},{2,3},{3,2},{6... | collective-permute-start | bytes 786440 | tf_op jit(solution)/shard_map/ppermute | solution.py:281
  68.8 15.8 %collective-permute-start.1 = (f32[128,512]{1,0:T(8,128)}, f32[128,512]{1,0:T(8,128)S(1)}, u32[]{:S(2)}, u32[]{:S(2)}) collective-permute-start(f32[128,512]{1,0:T(8,128)} %get-tuple-element.25), channel_id=1, source_target_pairs={{0,4},{1,5},{4,0},{5,1},{8,12},{9,13},{12,8},{13,9},{2,6},{3,7},{6... | collective-permute-start | bytes 786440 | tf_op jit(solution)/shard_map/ppermute | solution.py:281
  70.1 20.1 %collective-permute-start.2 = (f32[128,512]{1,0:T(8,128)}, f32[128,512]{1,0:T(8,128)S(1)}, u32[]{:S(2)}, u32[]{:S(2)}) collective-permute-start(f32[128,512]{1,0:T(8,128)} %get-tuple-element.26), channel_id=1, source_target_pairs={{0,5},{1,4},{4,1},{5,0},{8,13},{9,12},{12,9},{13,8},{2,7},{3,6},{6... | collective-permute-start | bytes 786440 | tf_op jit(solution)/shard_map/ppermute | solution.py:281
  70.5 19.7 %collective-permute-start.3 = (f32[128,512]{1,0:T(8,128)}, f32[128,512]{1,0:T(8,128)S(1)}, u32[]{:S(2)}, u32[]{:S(2)}) collective-permute-start(f32[128,512]{1,0:T(8,128)} %get-tuple-element.27), channel_id=1, source_target_pairs={{0,8},{1,9},{4,12},{5,13},{8,0},{9,1},{12,4},{13,5},{2,10},{3,11},... | collective-permute-start | bytes 786440 | tf_op jit(solution)/shard_map/ppermute | solution.py:281
  70.6 23.8 %collective-permute-start.4 = (f32[128,512]{1,0:T(8,128)}, f32[128,512]{1,0:T(8,128)S(1)}, u32[]{:S(2)}, u32[]{:S(2)}) collective-permute-start(f32[128,512]{1,0:T(8,128)} %get-tuple-element.28), channel_id=1, source_target_pairs={{0,9},{1,8},{4,13},{5,12},{8,1},{9,0},{12,5},{13,4},{2,11},{3,10},... | collective-permute-start | bytes 786440 | tf_op jit(solution)/shard_map/ppermute | solution.py:281
  73.2 40.0 %collective-permute-start.5 = (f32[128,512]{1,0:T(8,128)}, f32[128,512]{1,0:T(8,128)S(1)}, u32[]{:S(2)}, u32[]{:S(2)}) collective-permute-start(f32[128,512]{1,0:T(8,128)} %get-tuple-element.29), channel_id=1, source_target_pairs={{0,12},{1,13},{4,8},{5,9},{8,4},{9,5},{12,0},{13,1},{2,14},{3,15},... | collective-permute-start | bytes 786440 | tf_op jit(solution)/shard_map/ppermute | solution.py:281
  84.6 34.6 %collective-permute-start.6 = (f32[128,512]{1,0:T(8,128)}, f32[128,512]{1,0:T(8,128)S(1)}, u32[]{:S(2)}, u32[]{:S(2)}) collective-permute-start(f32[128,512]{1,0:T(8,128)} %get-tuple-element.30), channel_id=1, source_target_pairs={{0,13},{1,12},{4,9},{5,8},{8,5},{9,4},{12,1},{13,0},{2,15},{3,14},... | collective-permute-start | bytes 786440 | tf_op jit(solution)/shard_map/ppermute | solution.py:281
  119.8 0.9 copy-start
  120.8 0.9 copy-start.3
  156.1 16.5 %collective-permute-start.7 = (f32[1024,256]{1,0:T(8,128)S(1)}, f32[1024,256]{1,0:T(8,128)}, u32[]{:S(2)}, u32[]{:S(2)}) collective-permute-start(f32[1024,256]{1,0:T(8,128)S(1)} %broadcast_select_fusion.2), channel_id=1, source_target_pairs={{0,1},{1,4},{4,5},{5,8},{8,9},{9,12},{12,13},{13,15},{15,14},{14,1... | collective-permute-start | bytes 3145736 | tf_op jit(solution)/shard_map/ppermute | solution.py:329
  158.2 15.3 %collective-permute-start.8 = (f32[1024,256]{1,0:T(8,128)S(1)}, f32[1024,256]{1,0:T(8,128)}, u32[]{:S(2)}, u32[]{:S(2)}) collective-permute-start(f32[1024,256]{1,0:T(8,128)S(1)} %get-tuple-element.32), channel_id=1, source_target_pairs={{1,0},{4,1},{5,4},{8,5},{9,8},{12,9},{13,12},{15,13},{14,15},{11,1... | collective-permute-start | bytes 3145736 | tf_op jit(solution)/shard_map/ppermute | solution.py:329
  209.1 5.7 %collective-permute-start.9 = (f32[128,512]{1,0:T(8,128)S(1)}, f32[128,512]{1,0:T(8,128)S(1)}, u32[]{:S(2)}, u32[]{:S(2)}) collective-permute-start(f32[128,512]{1,0:T(8,128)S(1)} %get-tuple-element.34), channel_id=1, source_target_pairs={{0,1},{1,0},{4,5},{5,4},{8,9},{9,8},{12,13},{13,12},{2,3},{3,2},{6... | collective-permute-start | bytes 786440 | tf_op jit(solution)/shard_map/ppermute | solution.py:281
  210.1 15.3 %collective-permute-start.10 = (f32[128,512]{1,0:T(8,128)S(1)}, f32[128,512]{1,0:T(8,128)S(1)}, u32[]{:S(2)}, u32[]{:S(2)}) collective-permute-start(f32[128,512]{1,0:T(8,128)S(1)} %get-tuple-element.35), channel_id=1, source_target_pairs={{0,4},{1,5},{4,0},{5,1},{8,12},{9,13},{12,8},{13,9},{2,6},{3,7},{6... | collective-permute-start | bytes 786440 | tf_op jit(solution)/shard_map/ppermute | solution.py:281
  211.8 19.2 %collective-permute-start.11 = (f32[128,512]{1,0:T(8,128)S(1)}, f32[128,512]{1,0:T(8,128)S(1)}, u32[]{:S(2)}, u32[]{:S(2)}) collective-permute-start(f32[128,512]{1,0:T(8,128)S(1)} %get-tuple-element.36), channel_id=1, source_target_pairs={{0,5},{1,4},{4,1},{5,0},{8,13},{9,12},{12,9},{13,8},{2,7},{3,6},{6... | collective-permute-start | bytes 786440 | tf_op jit(solution)/shard_map/ppermute | solution.py:281
  211.8 19.2 %collective-permute-start.12 = (f32[128,512]{1,0:T(8,128)S(1)}, f32[128,512]{1,0:T(8,128)S(1)}, u32[]{:S(2)}, u32[]{:S(2)}) collective-permute-start(f32[128,512]{1,0:T(8,128)S(1)} %get-tuple-element.37), channel_id=1, source_target_pairs={{0,8},{1,9},{4,12},{5,13},{8,0},{9,1},{12,4},{13,5},{2,10},{3,11},... | collective-permute-start | bytes 786440 | tf_op jit(solution)/shard_map/ppermute | solution.py:281
  211.8 23.3 %collective-permute-start.13 = (f32[128,512]{1,0:T(8,128)S(1)}, f32[128,512]{1,0:T(8,128)S(1)}, u32[]{:S(2)}, u32[]{:S(2)}) collective-permute-start(f32[128,512]{1,0:T(8,128)S(1)} %get-tuple-element.38), channel_id=1, source_target_pairs={{0,9},{1,8},{4,13},{5,12},{8,1},{9,0},{12,5},{13,4},{2,11},{3,10},... | collective-permute-start | bytes 786440 | tf_op jit(solution)/shard_map/ppermute | solution.py:281
  214.8 45.8 %copy-start.6 = (f32[128,512]{1,0:T(8,128)}, f32[128,512]{1,0:T(8,128)S(1)}, u32[]{:S(2)}) copy-start(f32[128,512]{1,0:T(8,128)S(1)} %collective-permute-done.9.refs_1_) | copy-start | bytes 786436
  214.8 39.8 %collective-permute-start.14 = (f32[128,512]{1,0:T(8,128)S(1)}, f32[128,512]{1,0:T(8,128)S(1)}, u32[]{:S(2)}, u32[]{:S(2)}) collective-permute-start(f32[128,512]{1,0:T(8,128)S(1)} %get-tuple-element.39), channel_id=1, source_target_pairs={{0,12},{1,13},{4,8},{5,9},{8,4},{9,5},{12,0},{13,1},{2,14},{3,15},... | collective-permute-start | bytes 786440 | tf_op jit(solution)/shard_map/ppermute | solution.py:281
  225.4 35.2 %copy-start.7 = (f32[128,512]{1,0:T(8,128)}, f32[128,512]{1,0:T(8,128)S(1)}, u32[]{:S(2)}) copy-start(f32[128,512]{1,0:T(8,128)S(1)} %collective-permute-done.10.refs_2_) | copy-start | bytes 786436
  225.4 35.2 %collective-permute-start.15 = (f32[128,512]{1,0:T(8,128)S(1)}, f32[128,512]{1,0:T(8,128)S(1)}, u32[]{:S(2)}, u32[]{:S(2)}) collective-permute-start(f32[128,512]{1,0:T(8,128)S(1)} %get-tuple-element.40), channel_id=1, source_target_pairs={{0,13},{1,12},{4,9},{5,8},{8,5},{9,4},{12,1},{13,0},{2,15},{3,14},... | collective-permute-start | bytes 786440 | tf_op jit(solution)/shard_map/ppermute | solution.py:281
  231.0 29.6 %copy-start.8 = (f32[128,512]{1,0:T(8,128)}, f32[128,512]{1,0:T(8,128)S(1)}, u32[]{:S(2)}) copy-start(f32[128,512]{1,0:T(8,128)S(1)} %collective-permute-done.11.refs_3_) | copy-start | bytes 786436
  231.0 29.6 %copy-start.9 = (f32[128,512]{1,0:T(8,128)}, f32[128,512]{1,0:T(8,128)S(1)}, u32[]{:S(2)}) copy-start(f32[128,512]{1,0:T(8,128)S(1)} %collective-permute-done.12.refs_4_) | copy-start | bytes 786436
  235.1 25.5 %copy-start.10 = (f32[128,512]{1,0:T(8,128)}, f32[128,512]{1,0:T(8,128)S(1)}, u32[]{:S(2)}) copy-start(f32[128,512]{1,0:T(8,128)S(1)} %collective-permute-done.13.refs_5_) | copy-start | bytes 786436
  254.6 6.0 %copy-start.11 = (f32[128,512]{1,0:T(8,128)}, f32[128,512]{1,0:T(8,128)S(1)}, u32[]{:S(2)}) copy-start(f32[128,512]{1,0:T(8,128)S(1)} %collective-permute-done.14.refs_6_) | copy-start | bytes 786436
  (5 other events, 3.8 us)

commit v2 on v1

--- a/solution.py
+++ b/solution.py
@@ -100,60 +100,83 @@
 
 
 def pack_kernel(order_ref, x_ref, *refs):
-    outs, sem = refs[:-1], refs[-1]
-    copies = []
+    outs, held, in_sem, out_sem = refs[:-3], *refs[-3:]
+    count = len(outs)
+    loads, stores = [], []
     for i, out in enumerate(outs):
         for half in range(2):
             start = pl.multiple_of(order_ref[2 * i + half] * BLK, BLK)
-            copies.append(
+            loads.append(
                 pltpu.make_async_copy(
                     x_ref.at[:, pl.ds(start, BLK)],
-                    out.at[:, half * BLK : (half + 1) * BLK],
-                    sem.at[2 * i + half],
+                    held.at[i, :, half * BLK : (half + 1) * BLK],
+                    in_sem.at[2 * i + half],
                 )
             )
-    for copy in copies:
-        copy.start()
-    for copy in copies:
-        copy.wait()
+        stores.append(pltpu.make_async_copy(held.at[i], out, out_sem.at[i]))
+    farthest_first = [*range(1, count), 0]
+    for i in farthest_first:
+        loads[2 * i].start()
+        loads[2 * i + 1].start()
+    for i in farthest_first:
+        loads[2 * i].wait()
+        loads[2 * i + 1].wait()
+        stores[i].start()
+    for i in farthest_first:
+        stores[i].wait()
 
 
 def pack(order, x, count):
     rows = x.shape[0]
     piece = jax.ShapeDtypeStruct((rows, 2 * BLK), jnp.float32)
+    hbm = pl.BlockSpec(memory_space=pltpu.HBM)
     return pl.pallas_call(
         pack_kernel,
         out_shape=[piece] * count,
-        in_specs=[pl.BlockSpec(memory_space=pltpu.SMEM), pl.BlockSpec(memory_space=pl.ANY)],
-        out_specs=[pl.BlockSpec(memory_space=pl.ANY)] * count,
-        scratch_shapes=[pltpu.SemaphoreType.DMA((2 * count,))],
+        in_specs=[pl.BlockSpec(memory_space=pltpu.SMEM), hbm],
+        out_specs=[hbm] * count,
+        scratch_shapes=[
+            pltpu.VMEM((count, rows, 2 * BLK), jnp.float32),
+            pltpu.SemaphoreType.DMA((2 * count,)),
+            pltpu.SemaphoreType.DMA((count,)),
+        ],
         name="pack",
     )(order, x)
 
 
 def unpack_kernel(place_ref, *refs):
-    pieces, out_ref, sem = refs[:-2], refs[-2], refs[-1]
+    pieces, out_ref, held, in_sem, out_sem = refs[:-4], *refs[-4:]
     width = 2 * BLK
-    copies = []
+    loads, stores = [], []
     for i, piece in enumerate(pieces):
         start = pl.multiple_of(place_ref[i] * width, width)
-        copies.append(pltpu.make_async_copy(piece, out_ref.at[:, pl.ds(start, width)], sem.at[i]))
-    for copy in copies:
-        copy.start()
-    for copy in copies:
-        copy.wait()
+        loads.append(pltpu.make_async_copy(piece, held.at[i], in_sem.at[i]))
+        stores.append(
+            pltpu.make_async_copy(held.at[i], out_ref.at[:, pl.ds(start, width)], out_sem.at[i])
+        )
+    for load in loads:
+        load.start()
+    for load, store in zip(loads, stores):
+        load.wait()
+        store.start()
+    for store in stores:
+        store.wait()
 
 
 def unpack(place, pieces):
     rows, width = pieces[0].shape
     count = len(pieces)
+    hbm = pl.BlockSpec(memory_space=pltpu.HBM)
     return pl.pallas_call(
         unpack_kernel,
         out_shape=jax.ShapeDtypeStruct((rows, count * width), jnp.float32),
-        in_specs=[pl.BlockSpec(memory_space=pltpu.SMEM)]
-        + [pl.BlockSpec(memory_space=pl.ANY)] * count,
-        out_specs=pl.BlockSpec(memory_space=pl.ANY),
-        scratch_shapes=[pltpu.SemaphoreType.DMA((count,))],
+        in_specs=[pl.BlockSpec(memory_space=pltpu.SMEM)] + [hbm] * count,
+        out_specs=hbm,
+        scratch_shapes=[
+            pltpu.VMEM((count, rows, width), jnp.float32),
+            pltpu.SemaphoreType.DMA((count,)),
+            pltpu.SemaphoreType.DMA((count,)),
+        ],
         name="unpack",
     )(place, *pieces)
 
@@ -198,7 +221,7 @@
         functools.partial(first_kernel, count, int(bool(terms))),
         out_shape=[block, block],
         in_specs=[pl.BlockSpec(memory_space=pltpu.SMEM)]
-        + [pl.BlockSpec(memory_space=pl.ANY)] * count
+        + [pl.BlockSpec(memory_space=pltpu.HBM)] * count
         + [vmem] * len(terms),
         out_specs=[vmem, vmem],
         scratch_shapes=[
@@ -243,7 +266,7 @@
         functools.partial(last_kernel, count, int(bool(terms))),
         out_shape=[piece] * count,
         in_specs=[pl.BlockSpec(memory_space=pltpu.SMEM), vmem, vmem] + [vmem] * len(terms),
-        out_specs=[pl.BlockSpec(memory_space=pl.ANY)] * count,
+        out_specs=[pl.BlockSpec(memory_space=pltpu.HBM)] * count,
         scratch_shapes=[
             pltpu.VMEM((tokens, 2 * BLK), jnp.float32),
             pltpu.VMEM((2, BLK, 2 * BLK), jnp.float32),
@@ -267,8 +290,8 @@
     teams = token_group // pairs
     assert teams * pairs == token_group and pairs & (pairs - 1) == 0
     member = token_index % pairs
-    shifts = jnp.arange(pairs, dtype=jnp.int32)
-    partner = jnp.bitwise_xor(member, shifts)
+    shifts = [0] + list(range(pairs - 1, 0, -1))
+    partner = jnp.bitwise_xor(member, jnp.array(shifts, dtype=jnp.int32))
     backwards = column % 2 == 1
 
     def pair_of(member):
@@ -276,9 +299,9 @@
 
     def exchange(pieces):
         arrived = [pieces[0]]
-        for shift in range(1, pairs):
+        for shift, piece in zip(shifts[1:], pieces[1:]):
             route = [(t, t ^ shift) for t in range(token_group)]
-            arrived.append(lax.ppermute(pieces[shift], token_axes, route))
+            arrived.append(lax.ppermute(piece, token_axes, route))
         return arrived
 
     def added_up(upper, lower):

time: 327 us -> 204 us (0.62)
  the two profiles are of different devices: /device:TPU:19 before, /device:TPU:0 now
where the time goes in v2:
time: 204 us
  starting transfers between devices  76.2 us (37%)
  Pallas kernels  72.8 us (36%)
  waiting for transfers between devices  44.6 us (22%)
  local copies, waits for them, and re-layouts  7.67 us (4%)
  other arithmetic  2.48 us (1%)
    ppermute x14, starting transfers between devices, exchange(): arrived.append(lax.ppermute(piece, token_axes, route))  72.2 us
    ppermute x14, waiting for transfers between devices, exchange(): arrived.append(lax.ppermute(piece, token_axes, route))  41.3 us
    pallas_call x1, Pallas kernels, first_round(): pl.pallas_call(functools.partial(first_kernel, count, int(bool(terms))),...  33.3 us
    pallas_call x1, Pallas kernels, last_round(): pl.pallas_call(functools.partial(last_kernel, count, int(bool(terms))), o...  33.2 us
    unnamed x30, local copies, waits for them, and re-layouts  5.68 us
  transfers between devices with their start and end apart: 16, of which 10 were waited for; matrix products, arithmetic and copies ran while one was open for 0% of the time, Pallas kernels for 0%

profile of v2, /device:TPU:0, one launch (start us, length us, event | category | flops | bytes accessed | tf_op | source)
XLA Modules:
  0.0 204.1 jit_solution(17985517974993226622)
XLA Ops:
  2.9 3.2 %pack.1 = (f32[128,512]{1,0:T(8,128)}, f32[128,512]{1,0:T(8,128)}, f32[128,512]{1,0:T(8,128)}, f32[128,512]{1,0:T(8,128)}, f32[128,512]{1,0:T(8,128)}, /*index=5...) custom-call(s32[16]{0:T(128)} %select_n.67.order_ref, f32[128,4096]{1,0:T(8,128)} %x_ref.1), custom_call_target="tpu_custom_call" | custom-call | tf_op jit(solution)/shard_map/pack/pallas_call | solution.py:133
  6.1 4.6 %collective-permute-start = (f32[128,512]{1,0:T(8,128)}, f32[128,512]{1,0:T(8,128)S(1)}, u32[]{:S(2)}, u32[]{:S(2)}) collective-permute-start(f32[128,512]{1,0:T(8,128)} %get-tuple-element.24), channel_id=1, source_target_pairs={{0,13},{1,12},{4,9},{5,8},{8,5},{9,4},{12,1},{13,0},{2,15},{3,14},... | collective-permute-start | bytes 786440 | tf_op jit(solution)/shard_map/ppermute | solution.py:304
  11.7 2.2 %collective-permute-start.3 = (f32[128,512]{1,0:T(8,128)}, f32[128,512]{1,0:T(8,128)S(1)}, u32[]{:S(2)}, u32[]{:S(2)}) collective-permute-start(f32[128,512]{1,0:T(8,128)} %get-tuple-element.27), channel_id=1, source_target_pairs={{0,8},{1,9},{4,12},{5,13},{8,0},{9,1},{12,4},{13,5},{2,10},{3,11},... | collective-permute-start | bytes 786440 | tf_op jit(solution)/shard_map/ppermute | solution.py:304
  14.9 2.9 %collective-permute-done.refs_1_ = f32[128,512]{1,0:T(8,128)S(1)} collective-permute-done((f32[128,512]{1,0:T(8,128)}, f32[128,512]{1,0:T(8,128)S(1)}, u32[]{:S(2)}, u32[]{:S(2)}) %collective-permute-start) | collective-permute-done | bytes 262176 | tf_op jit(solution)/shard_map/ppermute | solution.py:304
  17.8 22.6 %collective-permute-start.5 = (f32[128,512]{1,0:T(8,128)}, f32[128,512]{1,0:T(8,128)S(1)}, u32[]{:S(2)}, u32[]{:S(2)}) collective-permute-start(f32[128,512]{1,0:T(8,128)} %get-tuple-element.29), channel_id=1, source_target_pairs={{0,4},{1,5},{4,0},{5,1},{8,12},{9,13},{12,8},{13,9},{2,6},{3,7},{6... | collective-permute-start | bytes 786440 | tf_op jit(solution)/shard_map/ppermute | solution.py:304
  40.5 10.7 %collective-permute-done.2.refs_3_ = f32[128,512]{1,0:T(8,128)S(1)} collective-permute-done((f32[128,512]{1,0:T(8,128)}, f32[128,512]{1,0:T(8,128)S(1)}, u32[]{:S(2)}, u32[]{:S(2)}) %collective-permute-start.2) | collective-permute-done | bytes 262176 | tf_op jit(solution)/shard_map/ppermute | solution.py:304
  51.2 5.8 %collective-permute-done.3.refs_4_ = f32[128,512]{1,0:T(8,128)S(1)} collective-permute-done((f32[128,512]{1,0:T(8,128)}, f32[128,512]{1,0:T(8,128)S(1)}, u32[]{:S(2)}, u32[]{:S(2)}) %collective-permute-start.3) | collective-permute-done | bytes 262176 | tf_op jit(solution)/shard_map/ppermute | solution.py:304
  56.9 1.8 collective-permute-done.5.refs_6_
  62.9 33.3 %first_round.1 = (f32[1024,256]{1,0:T(8,128)S(1)}, f32[1024,256]{1,0:T(8,128)S(1)}) custom-call(s32[8]{0:T(128)S(1)} %broadcast_xor_fusion.source_ref, f32[128,512]{1,0:T(8,128)S(1)} %copy-done, f32[128,512]{1,0:T(8,128)S(1)} %collective-permute-done.refs_1_, f32[128,512]{1,0:T(8,128)S(1)} %collective-permute-done.1.refs_2_, ...), custom_call_target="tpu_custom_call" | custom-call | tf_op jit(solution)/shard_map/first_round/pallas_call | solution.py:220
  96.4 2.7 %collective-permute-start.7 = (f32[1024,256]{1,0:T(8,128)S(1)}, f32[1024,256]{1,0:T(8,128)}, u32[]{:S(2)}, u32[]{:S(2)}) collective-permute-start(f32[1024,256]{1,0:T(8,128)S(1)} %broadcast_select_fusion.2), channel_id=1, source_target_pairs={{0,1},{1,4},{4,5},{5,8},{8,9},{9,12},{12,13},{13,15},{15,14},{14,1... | collective-permute-start | bytes 3145736 | tf_op jit(solution)/shard_map/ppermute | solution.py:352
  99.1 1.3 collective-permute-start.8
  100.5 3.2 %collective-permute-done.8 = f32[1024,256]{1,0:T(8,128)} collective-permute-done((f32[1024,256]{1,0:T(8,128)S(1)}, f32[1024,256]{1,0:T(8,128)}, u32[]{:S(2)}, u32[]{:S(2)}) %collective-permute-start.8) | collective-permute-done | bytes 1048608 | tf_op jit(solution)/shard_map/ppermute | solution.py:352
  103.7 1.4 broadcast_select_fusion
  105.2 33.2 %last_round.1 = (f32[128,512]{1,0:T(8,128)S(1)}, f32[128,512]{1,0:T(8,128)S(1)}, f32[128,512]{1,0:T(8,128)S(1)}, f32[128,512]{1,0:T(8,128)S(1)}, f32[128,512]{1,...) custom-call(s32[8]{0:T(128)S(1)} %broadcast_xor_fusion.source_ref, ...), custom_call_target="tpu_custom_call" | custom-call | tf_op jit(solution)/shard_map/last_round/pallas_call | solution.py:265
  139.1 13.3 %collective-permute-start.9 = (f32[128,512]{1,0:T(8,128)S(1)}, f32[128,512]{1,0:T(8,128)S(1)}, u32[]{:S(2)}, u32[]{:S(2)}) collective-permute-start(f32[128,512]{1,0:T(8,128)S(1)} %get-tuple-element.34), channel_id=1, source_target_pairs={{0,13},{1,12},{4,9},{5,8},{8,5},{9,4},{12,1},{13,0},{2,15},{3,14},... | collective-permute-start | bytes 786440 | tf_op jit(solution)/shard_map/ppermute | solution.py:304
  152.3 1.1 collective-permute-start.10
  153.4 1.6 collective-permute-start.12
  155.0 1.4 collective-permute-start.13
  156.5 2.6 %collective-permute-done.9.refs_1_ = f32[128,512]{1,0:T(8,128)S(1)} collective-permute-done((f32[128,512]{1,0:T(8,128)S(1)}, f32[128,512]{1,0:T(8,128)S(1)}, u32[]{:S(2)}, u32[]{:S(2)}) %collective-permute-start.9) | collective-permute-done | bytes 262176 | tf_op jit(solution)/shard_map/ppermute | solution.py:304
  159.0 23.4 %collective-permute-start.14 = (f32[128,512]{1,0:T(8,128)S(1)}, f32[128,512]{1,0:T(8,128)S(1)}, u32[]{:S(2)}, u32[]{:S(2)}) collective-permute-start(f32[128,512]{1,0:T(8,128)S(1)} %get-tuple-element.39), channel_id=1, source_target_pairs={{0,4},{1,5},{4,0},{5,1},{8,12},{9,13},{12,8},{13,9},{2,6},{3,7},{6... | collective-permute-start | bytes 786440 | tf_op jit(solution)/shard_map/ppermute | solution.py:304
  182.5 10.6 %collective-permute-done.11.refs_3_ = f32[128,512]{1,0:T(8,128)S(1)} collective-permute-done((f32[128,512]{1,0:T(8,128)S(1)}, f32[128,512]{1,0:T(8,128)S(1)}, u32[]{:S(2)}, u32[]{:S(2)}) %collective-permute-start.11) | collective-permute-done | bytes 262176 | tf_op jit(solution)/shard_map/ppermute | solution.py:304
  193.0 5.6 %collective-permute-done.12.refs_4_ = f32[128,512]{1,0:T(8,128)S(1)} collective-permute-done((f32[128,512]{1,0:T(8,128)S(1)}, f32[128,512]{1,0:T(8,128)S(1)}, u32[]{:S(2)}, u32[]{:S(2)}) %collective-permute-start.12) | collective-permute-done | bytes 262176 | tf_op jit(solution)/shard_map/ppermute | solution.py:304
  198.6 1.4 collective-permute-done.14.refs_6_
  200.8 3.1 %unpack.1 = f32[128,4096]{1,0:T(8,128)} custom-call(s32[8]{0:T(128)} %copy-done.13, f32[128,512]{1,0:T(8,128)} %copy-done.1, f32[128,512]{1,0:T(8,128)} %copy-done.6, f32[128,512]{1,0:T(8,128)} %copy-done.7, f32[128,512]{1,0:T(8,128)} %copy-done.8, f32[128,512]{1,0:T(8,128)} %copy-done.9, f32[128,512]{1,0:T(8,128)} %copy-done.10, f32[128,512]{1,0:T(8,128)} %copy-done.11, ...), custom_call_target="tpu_custom_call" | custom-call | tf_op jit(solution)/shard_map/unpack/pallas_call | solution.py:170
  (54 shorter events, 11.0 us)
Async XLA Ops:
  0.0 40.5 %copy-start.14 = (s32[8]{0:T(128)S(1)}, s32[8]{0:T(128)}, u32[]{:S(2)}) copy-start(s32[8]{0:T(128)} %constant.60.clone) | copy-start | bytes 100
  0.7 95.5 %copy-start.13 = (s32[8]{0:T(128)}, s32[8]{0:T(128)S(1)}, u32[]{:S(2)}) copy-start(s32[8]{0:T(128)S(1)} %get-tuple-element.42.place_ref) | copy-start | bytes 100
  6.1 11.6 %collective-permute-start = (f32[128,512]{1,0:T(8,128)}, f32[128,512]{1,0:T(8,128)S(1)}, u32[]{:S(2)}, u32[]{:S(2)}) collective-permute-start(f32[128,512]{1,0:T(8,128)} %get-tuple-element.24), channel_id=1, source_target_pairs={{0,13},{1,12},{4,9},{5,8},{8,5},{9,4},{12,1},{13,0},{2,15},{3,14},... | collective-permute-start | bytes 786440 | tf_op jit(solution)/shard_map/ppermute | solution.py:304
  10.7 29.7 %collective-permute-start.1 = (f32[128,512]{1,0:T(8,128)}, f32[128,512]{1,0:T(8,128)S(1)}, u32[]{:S(2)}, u32[]{:S(2)}) collective-permute-start(f32[128,512]{1,0:T(8,128)} %get-tuple-element.25), channel_id=1, source_target_pairs={{0,12},{1,13},{4,8},{5,9},{8,4},{9,5},{12,0},{13,1},{2,14},{3,15},... | collective-permute-start | bytes 786440 | tf_op jit(solution)/shard_map/ppermute | solution.py:304
  11.3 39.8 %collective-permute-start.2 = (f32[128,512]{1,0:T(8,128)}, f32[128,512]{1,0:T(8,128)S(1)}, u32[]{:S(2)}, u32[]{:S(2)}) collective-permute-start(f32[128,512]{1,0:T(8,128)} %get-tuple-element.26), channel_id=1, source_target_pairs={{0,9},{1,8},{4,13},{5,12},{8,1},{9,0},{12,5},{13,4},{2,11},{3,10},... | collective-permute-start | bytes 786440 | tf_op jit(solution)/shard_map/ppermute | solution.py:304
  11.7 45.2 %collective-permute-start.3 = (f32[128,512]{1,0:T(8,128)}, f32[128,512]{1,0:T(8,128)S(1)}, u32[]{:S(2)}, u32[]{:S(2)}) collective-permute-start(f32[128,512]{1,0:T(8,128)} %get-tuple-element.27), channel_id=1, source_target_pairs={{0,8},{1,9},{4,12},{5,13},{8,0},{9,1},{12,4},{13,5},{2,10},{3,11},... | collective-permute-start | bytes 786440 | tf_op jit(solution)/shard_map/ppermute | solution.py:304
  13.9 43.0 %collective-permute-start.4 = (f32[128,512]{1,0:T(8,128)}, f32[128,512]{1,0:T(8,128)S(1)}, u32[]{:S(2)}, u32[]{:S(2)}) collective-permute-start(f32[128,512]{1,0:T(8,128)} %get-tuple-element.28), channel_id=1, source_target_pairs={{0,5},{1,4},{4,1},{5,0},{8,13},{9,12},{12,9},{13,8},{2,7},{3,6},{6... | collective-permute-start | bytes 786440 | tf_op jit(solution)/shard_map/ppermute | solution.py:304
  17.8 40.9 %collective-permute-start.5 = (f32[128,512]{1,0:T(8,128)}, f32[128,512]{1,0:T(8,128)S(1)}, u32[]{:S(2)}, u32[]{:S(2)}) collective-permute-start(f32[128,512]{1,0:T(8,128)} %get-tuple-element.29), channel_id=1, source_target_pairs={{0,4},{1,5},{4,0},{5,1},{8,12},{9,13},{12,8},{13,9},{2,6},{3,7},{6... | collective-permute-start | bytes 786440 | tf_op jit(solution)/shard_map/ppermute | solution.py:304
  40.4 19.0 %collective-permute-start.6 = (f32[128,512]{1,0:T(8,128)}, f32[128,512]{1,0:T(8,128)S(1)}, u32[]{:S(2)}, u32[]{:S(2)}) collective-permute-start(f32[128,512]{1,0:T(8,128)} %get-tuple-element.30), channel_id=1, source_target_pairs={{0,1},{1,0},{4,5},{5,4},{8,9},{9,8},{12,13},{13,12},{2,3},{3,2},{6... | collective-permute-start | bytes 786440 | tf_op jit(solution)/shard_map/ppermute | solution.py:304
  60.1 0.9 copy-start
  96.4 4.1 %collective-permute-start.7 = (f32[1024,256]{1,0:T(8,128)S(1)}, f32[1024,256]{1,0:T(8,128)}, u32[]{:S(2)}, u32[]{:S(2)}) collective-permute-start(f32[1024,256]{1,0:T(8,128)S(1)} %broadcast_select_fusion.2), channel_id=1, source_target_pairs={{0,1},{1,4},{4,5},{5,8},{8,9},{9,12},{12,13},{13,15},{15,14},{14,1... | collective-permute-start | bytes 3145736 | tf_op jit(solution)/shard_map/ppermute | solution.py:352
  99.1 4.7 %collective-permute-start.8 = (f32[1024,256]{1,0:T(8,128)S(1)}, f32[1024,256]{1,0:T(8,128)}, u32[]{:S(2)}, u32[]{:S(2)}) collective-permute-start(f32[1024,256]{1,0:T(8,128)S(1)} %get-tuple-element.32), channel_id=1, source_target_pairs={{1,0},{4,1},{5,4},{8,5},{9,8},{12,9},{13,12},{15,13},{14,15},{11,1... | collective-permute-start | bytes 3145736 | tf_op jit(solution)/shard_map/ppermute | solution.py:352
  139.1 20.0 %collective-permute-start.9 = (f32[128,512]{1,0:T(8,128)S(1)}, f32[128,512]{1,0:T(8,128)S(1)}, u32[]{:S(2)}, u32[]{:S(2)}) collective-permute-start(f32[128,512]{1,0:T(8,128)S(1)} %get-tuple-element.34), channel_id=1, source_target_pairs={{0,13},{1,12},{4,9},{5,8},{8,5},{9,4},{12,1},{13,0},{2,15},{3,14},... | collective-permute-start | bytes 786440 | tf_op jit(solution)/shard_map/ppermute | solution.py:304
  152.3 30.1 %collective-permute-start.10 = (f32[128,512]{1,0:T(8,128)S(1)}, f32[128,512]{1,0:T(8,128)S(1)}, u32[]{:S(2)}, u32[]{:S(2)}) collective-permute-start(f32[128,512]{1,0:T(8,128)S(1)} %get-tuple-element.35), channel_id=1, source_target_pairs={{0,12},{1,13},{4,8},{5,9},{8,4},{9,5},{12,0},{13,1},{2,14},{3,15},... | collective-permute-start | bytes 786440 | tf_op jit(solution)/shard_map/ppermute | solution.py:304
  153.4 39.6 %collective-permute-start.11 = (f32[128,512]{1,0:T(8,128)S(1)}, f32[128,512]{1,0:T(8,128)S(1)}, u32[]{:S(2)}, u32[]{:S(2)}) collective-permute-start(f32[128,512]{1,0:T(8,128)S(1)} %get-tuple-element.36), channel_id=1, source_target_pairs={{0,9},{1,8},{4,13},{5,12},{8,1},{9,0},{12,5},{13,4},{2,11},{3,10},... | collective-permute-start | bytes 786440 | tf_op jit(solution)/shard_map/ppermute | solution.py:304
  153.4 45.2 %collective-permute-start.12 = (f32[128,512]{1,0:T(8,128)S(1)}, f32[128,512]{1,0:T(8,128)S(1)}, u32[]{:S(2)}, u32[]{:S(2)}) collective-permute-start(f32[128,512]{1,0:T(8,128)S(1)} %get-tuple-element.37), channel_id=1, source_target_pairs={{0,8},{1,9},{4,12},{5,13},{8,0},{9,1},{12,4},{13,5},{2,10},{3,11},... | collective-permute-start | bytes 786440 | tf_op jit(solution)/shard_map/ppermute | solution.py:304
  155.0 43.6 %collective-permute-start.13 = (f32[128,512]{1,0:T(8,128)S(1)}, f32[128,512]{1,0:T(8,128)S(1)}, u32[]{:S(2)}, u32[]{:S(2)}) collective-permute-start(f32[128,512]{1,0:T(8,128)S(1)} %get-tuple-element.38), channel_id=1, source_target_pairs={{0,5},{1,4},{4,1},{5,0},{8,13},{9,12},{12,9},{13,8},{2,7},{3,6},{6... | collective-permute-start | bytes 786440 | tf_op jit(solution)/shard_map/ppermute | solution.py:304
  159.0 41.0 %copy-start.6 = (f32[128,512]{1,0:T(8,128)}, f32[128,512]{1,0:T(8,128)S(1)}, u32[]{:S(2)}) copy-start(f32[128,512]{1,0:T(8,128)S(1)} %collective-permute-done.9.refs_1_) | copy-start | bytes 786436
  159.0 41.0 %collective-permute-start.14 = (f32[128,512]{1,0:T(8,128)S(1)}, f32[128,512]{1,0:T(8,128)S(1)}, u32[]{:S(2)}, u32[]{:S(2)}) collective-permute-start(f32[128,512]{1,0:T(8,128)S(1)} %get-tuple-element.39), channel_id=1, source_target_pairs={{0,4},{1,5},{4,0},{5,1},{8,12},{9,13},{12,8},{13,9},{2,6},{3,7},{6... | collective-permute-start | bytes 786440 | tf_op jit(solution)/shard_map/ppermute | solution.py:304
  182.4 17.6 %copy-start.7 = (f32[128,512]{1,0:T(8,128)}, f32[128,512]{1,0:T(8,128)S(1)}, u32[]{:S(2)}) copy-start(f32[128,512]{1,0:T(8,128)S(1)} %collective-permute-done.10.refs_2_) | copy-start | bytes 786436
  182.4 17.6 %collective-permute-start.15 = (f32[128,512]{1,0:T(8,128)S(1)}, f32[128,512]{1,0:T(8,128)S(1)}, u32[]{:S(2)}, u32[]{:S(2)}) collective-permute-start(f32[128,512]{1,0:T(8,128)S(1)} %get-tuple-element.40), channel_id=1, source_target_pairs={{0,1},{1,0},{4,5},{5,4},{8,9},{9,8},{12,13},{13,12},{2,3},{3,2},{6... | collective-permute-start | bytes 786440 | tf_op jit(solution)/shard_map/ppermute | solution.py:304
  193.0 7.1 %copy-start.8 = (f32[128,512]{1,0:T(8,128)}, f32[128,512]{1,0:T(8,128)S(1)}, u32[]{:S(2)}) copy-start(f32[128,512]{1,0:T(8,128)S(1)} %collective-permute-done.11.refs_3_) | copy-start | bytes 786436
  198.6 1.5 copy-start.9
  198.6 1.5 copy-start.10
  (7 other events, 5.5 us)

commit v3 on v2

--- a/solution.py
+++ b/solution.py
@@ -27,49 +27,84 @@
     return lax.broadcasted_iota(jnp.int32, shape, dim)
 
 
+def reciprocal(x):
+    guess = pl.reciprocal(x, approx=True)
+    return guess * (2.0 - x * guess)
+
+
 def eliminate(blocks):
     width = 2 * PANEL
+    shape = (SUBLANES, width)
     tiles = PANEL // SUBLANES
+    lines = range(SUBLANES)
     ident = jnp.where(iota2((PANEL, PANEL), 0) == iota2((PANEL, PANEL), 1), 1.0, 0.0).astype(jnp.float32)
-    parts = []
+    sub = iota2(shape, 0)
+    parts, outs = [], []
     for block in blocks:
         whole = jnp.concatenate([block, ident], axis=1)
         parts.append([whole[SUBLANES * v : SUBLANES * (v + 1)] for v in range(tiles)])
-    sub = iota2((SUBLANES, width), 0)
-    for j in range(PANEL):
-        home, line = divmod(j, SUBLANES)
+        outs.append([])
+    for q in range(tiles):
+        states = []
         for part in parts:
-            row = part[home][line : line + 1, :]
-            scaled = row / row[:, j : j + 1]
-            for v in range(home, tiles):
-                column = part[v][:, j : j + 1]
-                step = column * scaled
-                if v == home:
-                    step = jnp.where(sub > line, step, 0.0)
-                part[v] = part[v] - step
-    outs = []
-    on_diagonal = iota2((PANEL, width), 0) == iota2((PANEL, width), 1)
-    for part in parts:
-        whole = jnp.concatenate(part, axis=0)
-        pivots = jnp.sum(jnp.where(on_diagonal, whole, 0.0), axis=1, keepdims=True)
-        outs.append(whole[:, PANEL:] * lax.rsqrt(pivots))
-    return outs
-
-
-def inverse_factors(aug_ref):
+            columns = [
+                [
+                    jnp.broadcast_to(part[v][:, SUBLANES * q + j : SUBLANES * q + j + 1], shape)
+                    for j in lines
+                ]
+                for v in range(q, tiles)
+            ]
+            entry = [
+                [jnp.broadcast_to(columns[0][j][i : i + 1, :], shape) for j in range(i + 1)]
+                for i in lines
+            ]
+            rows = [jnp.broadcast_to(part[q][i : i + 1, :], shape) for i in lines]
+            states.append((columns, entry, rows, []))
+        for s in lines:
+            for columns, entry, rows, inverses in states:
+                inverse = reciprocal(entry[s][s])
+                inverses.append(inverse)
+                factors = {i: entry[i][s] * inverse for i in range(s + 1, SUBLANES)}
+                for i in range(s + 1, SUBLANES):
+                    for j in range(s + 1, i + 1):
+                        entry[i][j] = entry[i][j] - factors[i] * entry[j][s]
+                for i in range(s + 1, SUBLANES):
+                    rows[i] = rows[i] - factors[i] * rows[s]
+        for v in range(q + 1, tiles):
+            for part, (columns, entry, rows, inverses) in zip(parts, states):
+                factors = []
+                for s in lines:
+                    value = columns[v - q][s]
+                    for t in range(s):
+                        value = value - factors[t] * entry[s][t]
+                    factors.append(value * inverses[s])
+                for s in lines:
+                    part[v] = part[v] - factors[s] * rows[s]
+        for out, (columns, entry, rows, inverses) in zip(outs, states):
+            tile = rows[0] * lax.rsqrt(entry[0][0])
+            for i in lines[1:]:
+                tile = jnp.where(sub == i, rows[i] * lax.rsqrt(entry[i][i]), tile)
+            out.append(tile[:, PANEL:])
+    return [jnp.concatenate(out, axis=0) for out in outs]
+
+
+def inverse_factors(work_ref, inv_ref):
+    inv_ref[...] = jnp.zeros_like(inv_ref)
+    ident = jnp.where(iota2((PANEL, PANEL), 0) == iota2((PANEL, PANEL), 1), 1.0, 0.0).astype(jnp.float32)
     for p in range(BLK // PANEL):
         top = p * PANEL
         end = top + PANEL
-        blocks = [aug_ref[m, top:end, top:end] for m in range(2)]
-        invs = eliminate(blocks)
+        invs = eliminate([work_ref[m, top:end, top:end] for m in range(2)])
         for m in range(2):
-            rows = contract(invs[m], aug_ref[m, top:end, :], 1, 0)
-            aug_ref[m, top:end, BLK:] = rows[:, BLK:]
+            work_ref[m, top:end, top:end] = ident
+            rows = contract(invs[m], work_ref[m, top:end, :], 1, 0)
+            inv_ref[m, top:end, :end] = rows[:, :end]
             if end < BLK:
-                aug_ref[m, end:, :] = aug_ref[m, end:, :] - contract(rows[:, end:BLK], rows, 0, 0)
-
-
-def rotate_pair(upper_ref, lower_ref, cross, upper_sq, lower_sq, aug_ref):
+                work_ref[m, end:, top:end] = jnp.zeros((BLK - end, PANEL), jnp.float32)
+                work_ref[m, end:, :] = work_ref[m, end:, :] - contract(rows[:, end:], rows, 0, 0)
+
+
+def rotate_pair(upper_ref, lower_ref, cross, upper_sq, lower_sq, work_ref, inv_ref):
     square = (BLK, BLK)
     diagonal = iota2(square, 0) == iota2(square, 1)
     ident = jnp.where(diagonal, 1.0, 0.0).astype(jnp.float32)
@@ -77,17 +112,15 @@
         jnp.where(diagonal, jnp.broadcast_to(upper_sq, square), 0.0), axis=1, keepdims=True
     )
     corr = cross * lax.rsqrt(upper_sq + epsilon) * lax.rsqrt(lower_sq + epsilon)
-    aug_ref[0, :, :BLK] = ident + contract(corr, corr, 1, 1)
-    aug_ref[1, :, :BLK] = ident + contract(corr, corr, 0, 0)
-    aug_ref[0, :, BLK:] = ident
-    aug_ref[1, :, BLK:] = ident
-    inverse_factors(aug_ref)
+    work_ref[0] = ident + contract(corr, corr, 1, 1)
+    work_ref[1] = ident + contract(corr, corr, 0, 0)
+    inverse_factors(work_ref, inv_ref)
     upper = upper_ref[...]
     lower = lower_ref[...]
     mixed_upper = upper + contract(lower, corr, 1, 1)
     mixed_lower = lower - contract(upper, corr, 1, 0)
-    new_upper = contract(mixed_upper, aug_ref[0, :, BLK:], 1, 1)
-    new_lower = contract(mixed_lower, aug_ref[1, :, BLK:], 1, 1)
+    new_upper = contract(mixed_upper, inv_ref[0], 1, 1)
+    new_lower = contract(mixed_lower, inv_ref[1], 1, 1)
     return new_upper, new_lower
 
 
@@ -185,7 +218,7 @@
     pieces = refs[:count]
     refs = refs[count:]
     terms, refs = refs[: 3 * given], refs[3 * given :]
-    new_upper_ref, new_lower_ref, upper_ref, lower_ref, aug_ref, sem = refs
+    new_upper_ref, new_lower_ref, upper_ref, lower_ref, work_ref, inv_ref, sem = refs
     rows = pieces[0].shape[0]
     copies = []
     for i, piece in enumerate(pieces):
@@ -206,7 +239,9 @@
         cross, upper_sq, lower_sq = (term[...] for term in terms)
     else:
         cross, upper_sq, lower_sq = terms_of(upper_ref[...], lower_ref[...])
-    new_upper, new_lower = rotate_pair(upper_ref, lower_ref, cross, upper_sq, lower_sq, aug_ref)
+    new_upper, new_lower = rotate_pair(
+        upper_ref, lower_ref, cross, upper_sq, lower_sq, work_ref, inv_ref
+    )
     new_upper_ref[...] = new_upper
     new_lower_ref[...] = new_lower
 
@@ -227,7 +262,8 @@
         scratch_shapes=[
             pltpu.VMEM((tokens, BLK), jnp.float32),
             pltpu.VMEM((tokens, BLK), jnp.float32),
-            pltpu.VMEM((2, BLK, 2 * BLK), jnp.float32),
+            pltpu.VMEM((2, BLK, BLK), jnp.float32),
+            pltpu.VMEM((2, BLK, BLK), jnp.float32),
             pltpu.SemaphoreType.DMA((2 * count,)),
         ],
         compiler_params=pltpu.CompilerParams(vmem_limit_bytes=VMEM_LIMIT),
@@ -238,13 +274,15 @@
 def last_kernel(count, given, source_ref, upper_ref, lower_ref, *refs):
     terms, refs = refs[: 3 * given], refs[3 * given :]
     outs = refs[:count]
-    result_ref, aug_ref, sem = refs[count:]
+    result_ref, work_ref, inv_ref, sem = refs[count:]
     rows = outs[0].shape[0]
     if given:
         cross, upper_sq, lower_sq = (term[...] for term in terms)
     else:
         cross, upper_sq, lower_sq = terms_of(upper_ref[...], lower_ref[...])
-    new_upper, new_lower = rotate_pair(upper_ref, lower_ref, cross, upper_sq, lower_sq, aug_ref)
+    new_upper, new_lower = rotate_pair(
+        upper_ref, lower_ref, cross, upper_sq, lower_sq, work_ref, inv_ref
+    )
     result_ref[:, :BLK] = new_upper
     result_ref[:, BLK:] = new_lower
     copies = []
@@ -269,7 +307,8 @@
         out_specs=[pl.BlockSpec(memory_space=pltpu.HBM)] * count,
         scratch_shapes=[
             pltpu.VMEM((tokens, 2 * BLK), jnp.float32),
-            pltpu.VMEM((2, BLK, 2 * BLK), jnp.float32),
+            pltpu.VMEM((2, BLK, BLK), jnp.float32),
+            pltpu.VMEM((2, BLK, BLK), jnp.float32),
             pltpu.SemaphoreType.DMA((count,)),
         ],
         compiler_params=pltpu.CompilerParams(vmem_limit_bytes=VMEM_LIMIT),

time: 204 us -> 179 us (0.88)
  Pallas kernels: 72.8 us -> 47.8 us
    pallas_call x1, Pallas kernels: 33.3 us -> 20.8 us  [first_round(): pl.pallas_call(functools.partial(first_kernel, count, int(bool(terms))),...]
    pallas_call x1, Pallas kernels: 33.2 us -> 20.7 us  [last_round(): pl.pallas_call(functools.partial(last_kernel, count, int(bool(terms))), o...]
where the time goes in v3:
time: 179 us
  starting transfers between devices  76.2 us (43%)
  Pallas kernels  47.8 us (27%)
  waiting for transfers between devices  44.6 us (25%)
  local copies, waits for them, and re-layouts  7.67 us (4%)
  other arithmetic  2.48 us (1%)
    ppermute x14, starting transfers between devices, exchange(): arrived.append(lax.ppermute(piece, token_axes, route))  72.3 us
    ppermute x14, waiting for transfers between devices, exchange(): arrived.append(lax.ppermute(piece, token_axes, route))  41.2 us
    pallas_call x1, Pallas kernels, first_round(): pl.pallas_call(functools.partial(first_kernel, count, int(bool(terms))),...  20.8 us
    pallas_call x1, Pallas kernels, last_round(): pl.pallas_call(functools.partial(last_kernel, count, int(bool(terms))), o...  20.7 us
    unnamed x30, local copies, waits for them, and re-layouts  5.68 us
    ppermute x2, starting transfers between devices, along(): return lax.ppermute(block, all_axes, route)  3.97 us
  transfers between devices with their start and end apart: 16, of which 10 were waited for; matrix products, arithmetic and copies ran while one was open for 0% of the time, Pallas kernels for 0%

profile of v3, /device:TPU:0, one launch (start us, length us, event | category | flops | bytes accessed | tf_op | source)
XLA Modules:
  0.0 179.1 jit_solution(17941668502318944453)
XLA Ops:
  2.9 3.2 %pack.1 = (f32[128,512]{1,0:T(8,128)}, f32[128,512]{1,0:T(8,128)}, f32[128,512]{1,0:T(8,128)}, f32[128,512]{1,0:T(8,128)}, f32[128,512]{1,0:T(8,128)}, /*index=5...) custom-call(s32[16]{0:T(128)} %select_n.67.order_ref, f32[128,4096]{1,0:T(8,128)} %x_ref.1), custom_call_target="tpu_custom_call" | custom-call | tf_op jit(solution)/shard_map/pack/pallas_call | solution.py:166
  6.1 4.6 %collective-permute-start = (f32[128,512]{1,0:T(8,128)}, f32[128,512]{1,0:T(8,128)S(1)}, u32[]{:S(2)}, u32[]{:S(2)}) collective-permute-start(f32[128,512]{1,0:T(8,128)} %get-tuple-element.24), channel_id=1, source_target_pairs={{0,13},{1,12},{4,9},{5,8},{8,5},{9,4},{12,1},{13,0},{2,15},{3,14},... | collective-permute-start | bytes 786440 | tf_op jit(solution)/shard_map/ppermute | solution.py:343
  11.7 2.2 %collective-permute-start.3 = (f32[128,512]{1,0:T(8,128)}, f32[128,512]{1,0:T(8,128)S(1)}, u32[]{:S(2)}, u32[]{:S(2)}) collective-permute-start(f32[128,512]{1,0:T(8,128)} %get-tuple-element.27), channel_id=1, source_target_pairs={{0,8},{1,9},{4,12},{5,13},{8,0},{9,1},{12,4},{13,5},{2,10},{3,11},... | collective-permute-start | bytes 786440 | tf_op jit(solution)/shard_map/ppermute | solution.py:343
  14.9 2.9 %collective-permute-done.refs_1_ = f32[128,512]{1,0:T(8,128)S(1)} collective-permute-done((f32[128,512]{1,0:T(8,128)}, f32[128,512]{1,0:T(8,128)S(1)}, u32[]{:S(2)}, u32[]{:S(2)}) %collective-permute-start) | collective-permute-done | bytes 262176 | tf_op jit(solution)/shard_map/ppermute | solution.py:343
  17.8 22.6 %collective-permute-start.5 = (f32[128,512]{1,0:T(8,128)}, f32[128,512]{1,0:T(8,128)S(1)}, u32[]{:S(2)}, u32[]{:S(2)}) collective-permute-start(f32[128,512]{1,0:T(8,128)} %get-tuple-element.29), channel_id=1, source_target_pairs={{0,4},{1,5},{4,0},{5,1},{8,12},{9,13},{12,8},{13,9},{2,6},{3,7},{6... | collective-permute-start | bytes 786440 | tf_op jit(solution)/shard_map/ppermute | solution.py:343
  40.5 10.7 %collective-permute-done.2.refs_3_ = f32[128,512]{1,0:T(8,128)S(1)} collective-permute-done((f32[128,512]{1,0:T(8,128)}, f32[128,512]{1,0:T(8,128)S(1)}, u32[]{:S(2)}, u32[]{:S(2)}) %collective-permute-start.2) | collective-permute-done | bytes 262176 | tf_op jit(solution)/shard_map/ppermute | solution.py:343
  51.2 5.8 %collective-permute-done.3.refs_4_ = f32[128,512]{1,0:T(8,128)S(1)} collective-permute-done((f32[128,512]{1,0:T(8,128)}, f32[128,512]{1,0:T(8,128)S(1)}, u32[]{:S(2)}, u32[]{:S(2)}) %collective-permute-start.3) | collective-permute-done | bytes 262176 | tf_op jit(solution)/shard_map/ppermute | solution.py:343
  56.9 1.8 collective-permute-done.5.refs_6_
  62.9 20.8 %first_round.1 = (f32[1024,256]{1,0:T(8,128)S(1)}, f32[1024,256]{1,0:T(8,128)S(1)}) custom-call(s32[8]{0:T(128)S(1)} %broadcast_xor_fusion.source_ref, f32[128,512]{1,0:T(8,128)S(1)} %copy-done, f32[128,512]{1,0:T(8,128)S(1)} %collective-permute-done.refs_1_, f32[128,512]{1,0:T(8,128)S(1)} %collective-permute-done.1.refs_2_, ...), custom_call_target="tpu_custom_call" | custom-call | tf_op jit(solution)/shard_map/first_round/pallas_call | solution.py:255
  83.9 2.7 %collective-permute-start.7 = (f32[1024,256]{1,0:T(8,128)S(1)}, f32[1024,256]{1,0:T(8,128)}, u32[]{:S(2)}, u32[]{:S(2)}) collective-permute-start(f32[1024,256]{1,0:T(8,128)S(1)} %broadcast_select_fusion.2), channel_id=1, source_target_pairs={{0,1},{1,4},{4,5},{5,8},{8,9},{9,12},{12,13},{13,15},{15,14},{14,1... | collective-permute-start | bytes 3145736 | tf_op jit(solution)/shard_map/ppermute | solution.py:391
  86.6 1.3 collective-permute-start.8
  88.0 3.2 %collective-permute-done.8 = f32[1024,256]{1,0:T(8,128)} collective-permute-done((f32[1024,256]{1,0:T(8,128)S(1)}, f32[1024,256]{1,0:T(8,128)}, u32[]{:S(2)}, u32[]{:S(2)}) %collective-permute-start.8) | collective-permute-done | bytes 1048608 | tf_op jit(solution)/shard_map/ppermute | solution.py:391
  91.2 1.4 broadcast_select_fusion
  92.7 20.7 %last_round.1 = (f32[128,512]{1,0:T(8,128)S(1)}, f32[128,512]{1,0:T(8,128)S(1)}, f32[128,512]{1,0:T(8,128)S(1)}, f32[128,512]{1,0:T(8,128)S(1)}, f32[128,512]{1,...) custom-call(s32[8]{0:T(128)S(1)} %broadcast_xor_fusion.source_ref, ...), custom_call_target="tpu_custom_call" | custom-call | tf_op jit(solution)/shard_map/last_round/pallas_call | solution.py:303
  114.1 13.3 %collective-permute-start.9 = (f32[128,512]{1,0:T(8,128)S(1)}, f32[128,512]{1,0:T(8,128)S(1)}, u32[]{:S(2)}, u32[]{:S(2)}) collective-permute-start(f32[128,512]{1,0:T(8,128)S(1)} %get-tuple-element.34), channel_id=1, source_target_pairs={{0,13},{1,12},{4,9},{5,8},{8,5},{9,4},{12,1},{13,0},{2,15},{3,14},... | collective-permute-start | bytes 786440 | tf_op jit(solution)/shard_map/ppermute | solution.py:343
  127.3 1.1 collective-permute-start.10
  128.4 1.6 collective-permute-start.12
  130.0 1.4 collective-permute-start.13
  131.5 2.6 %collective-permute-done.9.refs_1_ = f32[128,512]{1,0:T(8,128)S(1)} collective-permute-done((f32[128,512]{1,0:T(8,128)S(1)}, f32[128,512]{1,0:T(8,128)S(1)}, u32[]{:S(2)}, u32[]{:S(2)}) %collective-permute-start.9) | collective-permute-done | bytes 262176 | tf_op jit(solution)/shard_map/ppermute | solution.py:343
  134.0 23.4 %collective-permute-start.14 = (f32[128,512]{1,0:T(8,128)S(1)}, f32[128,512]{1,0:T(8,128)S(1)}, u32[]{:S(2)}, u32[]{:S(2)}) collective-permute-start(f32[128,512]{1,0:T(8,128)S(1)} %get-tuple-element.39), channel_id=1, source_target_pairs={{0,4},{1,5},{4,0},{5,1},{8,12},{9,13},{12,8},{13,9},{2,6},{3,7},{6... | collective-permute-start | bytes 786440 | tf_op jit(solution)/shard_map/ppermute | solution.py:343
  157.5 10.5 %collective-permute-done.11.refs_3_ = f32[128,512]{1,0:T(8,128)S(1)} collective-permute-done((f32[128,512]{1,0:T(8,128)S(1)}, f32[128,512]{1,0:T(8,128)S(1)}, u32[]{:S(2)}, u32[]{:S(2)}) %collective-permute-start.11) | collective-permute-done | bytes 262176 | tf_op jit(solution)/shard_map/ppermute | solution.py:343
  168.0 5.6 %collective-permute-done.12.refs_4_ = f32[128,512]{1,0:T(8,128)S(1)} collective-permute-done((f32[128,512]{1,0:T(8,128)S(1)}, f32[128,512]{1,0:T(8,128)S(1)}, u32[]{:S(2)}, u32[]{:S(2)}) %collective-permute-start.12) | collective-permute-done | bytes 262176 | tf_op jit(solution)/shard_map/ppermute | solution.py:343
  173.6 1.4 collective-permute-done.14.refs_6_
  175.8 3.1 %unpack.1 = f32[128,4096]{1,0:T(8,128)} custom-call(s32[8]{0:T(128)} %copy-done.13, f32[128,512]{1,0:T(8,128)} %copy-done.1, f32[128,512]{1,0:T(8,128)} %copy-done.6, f32[128,512]{1,0:T(8,128)} %copy-done.7, f32[128,512]{1,0:T(8,128)} %copy-done.8, f32[128,512]{1,0:T(8,128)} %copy-done.9, f32[128,512]{1,0:T(8,128)} %copy-done.10, f32[128,512]{1,0:T(8,128)} %copy-done.11, ...), custom_call_target="tpu_custom_call" | custom-call | tf_op jit(solution)/shard_map/unpack/pallas_call | solution.py:203
  (54 shorter events, 11.0 us)
Async XLA Ops:
  0.0 40.5 %copy-start.14 = (s32[8]{0:T(128)S(1)}, s32[8]{0:T(128)}, u32[]{:S(2)}) copy-start(s32[8]{0:T(128)} %constant.60.clone) | copy-start | bytes 100
  0.7 83.0 %copy-start.13 = (s32[8]{0:T(128)}, s32[8]{0:T(128)S(1)}, u32[]{:S(2)}) copy-start(s32[8]{0:T(128)S(1)} %get-tuple-element.42.place_ref) | copy-start | bytes 100
  6.1 11.6 %collective-permute-start = (f32[128,512]{1,0:T(8,128)}, f32[128,512]{1,0:T(8,128)S(1)}, u32[]{:S(2)}, u32[]{:S(2)}) collective-permute-start(f32[128,512]{1,0:T(8,128)} %get-tuple-element.24), channel_id=1, source_target_pairs={{0,13},{1,12},{4,9},{5,8},{8,5},{9,4},{12,1},{13,0},{2,15},{3,14},... | collective-permute-start | bytes 786440 | tf_op jit(solution)/shard_map/ppermute | solution.py:343
  10.7 29.7 %collective-permute-start.1 = (f32[128,512]{1,0:T(8,128)}, f32[128,512]{1,0:T(8,128)S(1)}, u32[]{:S(2)}, u32[]{:S(2)}) collective-permute-start(f32[128,512]{1,0:T(8,128)} %get-tuple-element.25), channel_id=1, source_target_pairs={{0,12},{1,13},{4,8},{5,9},{8,4},{9,5},{12,0},{13,1},{2,14},{3,15},... | collective-permute-start | bytes 786440 | tf_op jit(solution)/shard_map/ppermute | solution.py:343
  11.3 39.8 %collective-permute-start.2 = (f32[128,512]{1,0:T(8,128)}, f32[128,512]{1,0:T(8,128)S(1)}, u32[]{:S(2)}, u32[]{:S(2)}) collective-permute-start(f32[128,512]{1,0:T(8,128)} %get-tuple-element.26), channel_id=1, source_target_pairs={{0,9},{1,8},{4,13},{5,12},{8,1},{9,0},{12,5},{13,4},{2,11},{3,10},... | collective-permute-start | bytes 786440 | tf_op jit(solution)/shard_map/ppermute | solution.py:343
  11.7 45.2 %collective-permute-start.3 = (f32[128,512]{1,0:T(8,128)}, f32[128,512]{1,0:T(8,128)S(1)}, u32[]{:S(2)}, u32[]{:S(2)}) collective-permute-start(f32[128,512]{1,0:T(8,128)} %get-tuple-element.27), channel_id=1, source_target_pairs={{0,8},{1,9},{4,12},{5,13},{8,0},{9,1},{12,4},{13,5},{2,10},{3,11},... | collective-permute-start | bytes 786440 | tf_op jit(solution)/shard_map/ppermute | solution.py:343
  13.9 43.0 %collective-permute-start.4 = (f32[128,512]{1,0:T(8,128)}, f32[128,512]{1,0:T(8,128)S(1)}, u32[]{:S(2)}, u32[]{:S(2)}) collective-permute-start(f32[128,512]{1,0:T(8,128)} %get-tuple-element.28), channel_id=1, source_target_pairs={{0,5},{1,4},{4,1},{5,0},{8,13},{9,12},{12,9},{13,8},{2,7},{3,6},{6... | collective-permute-start | bytes 786440 | tf_op jit(solution)/shard_map/ppermute | solution.py:343
  17.8 40.9 %collective-permute-start.5 = (f32[128,512]{1,0:T(8,128)}, f32[128,512]{1,0:T(8,128)S(1)}, u32[]{:S(2)}, u32[]{:S(2)}) collective-permute-start(f32[128,512]{1,0:T(8,128)} %get-tuple-element.29), channel_id=1, source_target_pairs={{0,4},{1,5},{4,0},{5,1},{8,12},{9,13},{12,8},{13,9},{2,6},{3,7},{6... | collective-permute-start | bytes 786440 | tf_op jit(solution)/shard_map/ppermute | solution.py:343
  40.4 19.0 %collective-permute-start.6 = (f32[128,512]{1,0:T(8,128)}, f32[128,512]{1,0:T(8,128)S(1)}, u32[]{:S(2)}, u32[]{:S(2)}) collective-permute-start(f32[128,512]{1,0:T(8,128)} %get-tuple-element.30), channel_id=1, source_target_pairs={{0,1},{1,0},{4,5},{5,4},{8,9},{9,8},{12,13},{13,12},{2,3},{3,2},{6... | collective-permute-start | bytes 786440 | tf_op jit(solution)/shard_map/ppermute | solution.py:343
  60.1 0.9 copy-start
  83.9 4.1 %collective-permute-start.7 = (f32[1024,256]{1,0:T(8,128)S(1)}, f32[1024,256]{1,0:T(8,128)}, u32[]{:S(2)}, u32[]{:S(2)}) collective-permute-start(f32[1024,256]{1,0:T(8,128)S(1)} %broadcast_select_fusion.2), channel_id=1, source_target_pairs={{0,1},{1,4},{4,5},{5,8},{8,9},{9,12},{12,13},{13,15},{15,14},{14,1... | collective-permute-start | bytes 3145736 | tf_op jit(solution)/shard_map/ppermute | solution.py:391
  86.6 4.7 %collective-permute-start.8 = (f32[1024,256]{1,0:T(8,128)S(1)}, f32[1024,256]{1,0:T(8,128)}, u32[]{:S(2)}, u32[]{:S(2)}) collective-permute-start(f32[1024,256]{1,0:T(8,128)S(1)} %get-tuple-element.32), channel_id=1, source_target_pairs={{1,0},{4,1},{5,4},{8,5},{9,8},{12,9},{13,12},{15,13},{14,15},{11,1... | collective-permute-start | bytes 3145736 | tf_op jit(solution)/shard_map/ppermute | solution.py:391
  114.1 19.9 %collective-permute-start.9 = (f32[128,512]{1,0:T(8,128)S(1)}, f32[128,512]{1,0:T(8,128)S(1)}, u32[]{:S(2)}, u32[]{:S(2)}) collective-permute-start(f32[128,512]{1,0:T(8,128)S(1)} %get-tuple-element.34), channel_id=1, source_target_pairs={{0,13},{1,12},{4,9},{5,8},{8,5},{9,4},{12,1},{13,0},{2,15},{3,14},... | collective-permute-start | bytes 786440 | tf_op jit(solution)/shard_map/ppermute | solution.py:343
  127.3 30.1 %collective-permute-start.10 = (f32[128,512]{1,0:T(8,128)S(1)}, f32[128,512]{1,0:T(8,128)S(1)}, u32[]{:S(2)}, u32[]{:S(2)}) collective-permute-start(f32[128,512]{1,0:T(8,128)S(1)} %get-tuple-element.35), channel_id=1, source_target_pairs={{0,12},{1,13},{4,8},{5,9},{8,4},{9,5},{12,0},{13,1},{2,14},{3,15},... | collective-permute-start | bytes 786440 | tf_op jit(solution)/shard_map/ppermute | solution.py:343
  128.4 39.6 %collective-permute-start.11 = (f32[128,512]{1,0:T(8,128)S(1)}, f32[128,512]{1,0:T(8,128)S(1)}, u32[]{:S(2)}, u32[]{:S(2)}) collective-permute-start(f32[128,512]{1,0:T(8,128)S(1)} %get-tuple-element.36), channel_id=1, source_target_pairs={{0,9},{1,8},{4,13},{5,12},{8,1},{9,0},{12,5},{13,4},{2,11},{3,10},... | collective-permute-start | bytes 786440 | tf_op jit(solution)/shard_map/ppermute | solution.py:343
  128.4 45.2 %collective-permute-start.12 = (f32[128,512]{1,0:T(8,128)S(1)}, f32[128,512]{1,0:T(8,128)S(1)}, u32[]{:S(2)}, u32[]{:S(2)}) collective-permute-start(f32[128,512]{1,0:T(8,128)S(1)} %get-tuple-element.37), channel_id=1, source_target_pairs={{0,8},{1,9},{4,12},{5,13},{8,0},{9,1},{12,4},{13,5},{2,10},{3,11},... | collective-permute-start | bytes 786440 | tf_op jit(solution)/shard_map/ppermute | solution.py:343
  130.0 43.6 %collective-permute-start.13 = (f32[128,512]{1,0:T(8,128)S(1)}, f32[128,512]{1,0:T(8,128)S(1)}, u32[]{:S(2)}, u32[]{:S(2)}) collective-permute-start(f32[128,512]{1,0:T(8,128)S(1)} %get-tuple-element.38), channel_id=1, source_target_pairs={{0,5},{1,4},{4,1},{5,0},{8,13},{9,12},{12,9},{13,8},{2,7},{3,6},{6... | collective-permute-start | bytes 786440 | tf_op jit(solution)/shard_map/ppermute | solution.py:343
  134.0 41.0 %copy-start.6 = (f32[128,512]{1,0:T(8,128)}, f32[128,512]{1,0:T(8,128)S(1)}, u32[]{:S(2)}) copy-start(f32[128,512]{1,0:T(8,128)S(1)} %collective-permute-done.9.refs_1_) | copy-start | bytes 786436
  134.0 41.0 %collective-permute-start.14 = (f32[128,512]{1,0:T(8,128)S(1)}, f32[128,512]{1,0:T(8,128)S(1)}, u32[]{:S(2)}, u32[]{:S(2)}) collective-permute-start(f32[128,512]{1,0:T(8,128)S(1)} %get-tuple-element.39), channel_id=1, source_target_pairs={{0,4},{1,5},{4,0},{5,1},{8,12},{9,13},{12,8},{13,9},{2,6},{3,7},{6... | collective-permute-start | bytes 786440 | tf_op jit(solution)/shard_map/ppermute | solution.py:343
  157.5 17.6 %copy-start.7 = (f32[128,512]{1,0:T(8,128)}, f32[128,512]{1,0:T(8,128)S(1)}, u32[]{:S(2)}) copy-start(f32[128,512]{1,0:T(8,128)S(1)} %collective-permute-done.10.refs_2_) | copy-start | bytes 786436
  157.5 17.6 %collective-permute-start.15 = (f32[128,512]{1,0:T(8,128)S(1)}, f32[128,512]{1,0:T(8,128)S(1)}, u32[]{:S(2)}, u32[]{:S(2)}) collective-permute-start(f32[128,512]{1,0:T(8,128)S(1)} %get-tuple-element.40), channel_id=1, source_target_pairs={{0,1},{1,0},{4,5},{5,4},{8,9},{9,8},{12,13},{13,12},{2,3},{3,2},{6... | collective-permute-start | bytes 786440 | tf_op jit(solution)/shard_map/ppermute | solution.py:343
  168.0 7.1 %copy-start.8 = (f32[128,512]{1,0:T(8,128)}, f32[128,512]{1,0:T(8,128)S(1)}, u32[]{:S(2)}) copy-start(f32[128,512]{1,0:T(8,128)S(1)} %collective-permute-done.11.refs_3_) | copy-start | bytes 786436
  173.6 1.5 copy-start.9
  173.6 1.5 copy-start.10
  (7 other events, 5.5 us)
